TPU v7x, 256 devices: a whole 4x4x8 slice. The times are simulated.
256 devices in a mesh: leaf: 64 (over z, x, core), row: 4 (over y).
Axes of the slice: x: 4, y: 4, z: 8, core: 2. Of those that a mesh axis runs over, the one named last changes fastest.
Arguments:
- leaf_fronts: float32 [128, 8192, 512], P('leaf', 'row'), may hold values from -6 to 6
- front_rows: int32 [128], P('leaf'), may hold values from 768 to 8192, as said below
- parent_of: int32 [128], replicated, may hold values from 0 to 63, as said below
- column_map: int32 [128, 256], replicated, may hold values from 0 to 511, as said below
- parent_rows: float32 [64, 1024, 512], P('leaf', 'row'), may hold values from -6 to 6
Outputs:
- leaf_factor: float32 [128, 256, 512], P('leaf', None, 'row')
- parent_factor: float32 [64, 512, 512], P('leaf', None, 'row')
Inputs may be any that keep to these rules, and one draw needn't show every extreme that they name: `front_rows`: each leaf front has at least 1.5 times as many live rows as columns; some front has all 8192 live and some exactly the fewest. `parent_of`: the parent of leaf front c is within 2 of c // 2, and some front's parent is exactly 2 away. `column_map`: the 256 entries of a row are distinct.
All inputs are finite; a program needn't handle non-finite values.
Results may differ from a plain program's by a relative error of at most 0.0003.
Values sent between devices are 32-bit elements; how exact they have to be, the bound alone decides.
A program may use at most 64 MiB of HBM per device.

v0:
```python
import jax
import jax.numpy as jnp
from jax import lax
from jax.sharding import PartitionSpec as P

W = 256
REACH = 2


HIGHEST = lax.Precision.HIGHEST


def passed_along(value, axis, steps):
    count = lax.axis_size(axis)
    initial, last = (max(0, -steps), min(count, count - steps))
    return lax.ppermute(value, axis, [(source, source + steps) for source in range(initial, last)])


def child_term(summed, fragment, front_index, valid, parent_of, column_map, owner):

    def assemble(running):
        placed = jnp.zeros((fragment.shape[0], running.shape[1]), jnp.float32)
        placed = placed.at[:, column_map[front_index]].set(fragment)
        return running + jnp.dot(placed.T, placed, precision=HIGHEST)

    matches = jnp.logical_and(valid, parent_of[front_index] == owner)
    return lax.cond(matches, assemble, lambda running: running, summed)


def add_arrivals(children, arrived, offset, owner, leaf_devices, kid_count, parent_of, column_map):
    source = owner - offset
    valid = jnp.logical_and(source >= 0, source < leaf_devices)
    for position in range(kid_count):
        front_index = jnp.clip(source * kid_count + position, 0, leaf_devices * kid_count - 1)
        children = child_term(
            children, arrived[position], front_index, valid, parent_of, column_map, owner
        )
    return children


def per_device(leaf_fronts, front_rows, parent_of, column_map, parent_rows):
    kid_count, row_count, front_width = leaf_fronts.shape
    row_devices = lax.axis_size("row")
    leaf_devices = lax.axis_size("leaf")
    row_place = lax.axis_index("row")
    owner = lax.axis_index("leaf")
    total_rows = row_count * row_devices
    positions = row_place * row_count + jnp.arange(row_count, dtype=jnp.int32)
    live = positions[None, :, None] < front_rows[:, None, None]
    masked = jnp.where(live, leaf_fronts, 0.0)
    local_gram = jnp.einsum("kra,krb->kab", masked, masked, precision=HIGHEST) / total_rows
    leaf_gram = lax.psum(local_gram, "row")
    upper = jnp.swapaxes(jnp.linalg.cholesky(leaf_gram), 1, 2)
    share = front_width // row_devices
    leaf_factor = lax.dynamic_slice_in_dim(upper[:, :W, :], row_place * share, share, 2)
    contribution = upper[:, W:, W:]
    quarter = contribution.shape[1] // row_devices
    mine = lax.dynamic_slice_in_dim(contribution, row_place * quarter, quarter, 1)
    own_rows = parent_rows[0]
    parent_width = own_rows.shape[1]
    own_total = own_rows.shape[0] * row_devices
    own_gram = jnp.dot(own_rows.T, own_rows, precision=HIGHEST) / own_total
    children = jnp.zeros((parent_width, parent_width), jnp.float32)
    children = add_arrivals(
        children, mine, 0, owner, leaf_devices, kid_count, parent_of, column_map
    )
    for offset in range(-REACH, REACH + 1):
        if offset != 0:
            arrived = passed_along(mine, "leaf", offset)
            children = add_arrivals(
                children, arrived, offset, owner, leaf_devices, kid_count, parent_of, column_map
            )
    parent_gram = lax.psum(own_gram + children, "row")
    parent_upper = jnp.linalg.cholesky(parent_gram).T
    parent_share = parent_width // row_devices
    parent_factor = lax.dynamic_slice_in_dim(
        parent_upper, row_place * parent_share, parent_share, 1
    )
    return (leaf_factor, parent_factor[None])


def solution(mesh):
    return jax.shard_map(
        per_device,
        mesh=mesh,
        in_specs=(P("leaf", "row", None), P("leaf"), P(), P(), P("leaf", "row", None)),
        out_specs=(P("leaf", None, "row"), P("leaf", None, "row")),
        check_vma=False,
    )
```

profile of v0, /device:TPU:2, one launch (start us, length us, event | category | flops | bytes accessed | tf_op | source)
XLA Modules:
  0.0 465.5 jit_solution(1899070861939877477)
XLA Ops:
  8.0 23.0 %fusion.45 = f32[2,512,512]{1,2,0:T(8,128)} fusion(f32[2,2048,512]{2,1,0:T(8,128)} %param.25, pred[2,2048]{1,0:T(4,128)(4,1)S(1)} %broadcast_compare_fusion), kind=kOutput, calls=%fused_computation.76 | convolution fusion | flops 12887523328 | bytes 10489856 | tf_op jit(solution)/shard_map/kra,krb->kab/dot_general | solution.py:51
  32.7 65.3 %all-reduce.5.cloned.1.call-done = f32[2,512,512]{1,2,0:T(8,128)} async-done(((f32[2,512,512]{1,2,0:T(8,128)}), f32[2,512,512]{1,2,0:T(8,128)}) %all-reduce.5.cloned.1.call-update) | async-done | bytes 2097168 | tf_op jit(solution)/shard_map/psum | solution.py:52
  98.0 3.0 copy.47
  101.1 2.1 fusion.44
  104.5 23.5 %custom-call.58 = f32[2,128,128]{2,1,0:T(8,128)S(1)} custom-call(f32[2,128,128]{2,1,0:T(8,128)S(1)} %cholesky.534), custom_call_target="Cholesky" | custom-call | tf_op jit(solution)/shard_map/jit(cholesky)/cholesky | solution.py:53
  128.0 19.7 %custom-call.59 = f32[2,1,128,128]{2,3,1,0:T(8,128)S(1)} custom-call(f32[2,1,128,128]{3,2,1,0:T(8,128)S(1)} %select_bitcast_fusion.3), custom_call_target="InvertDiagBlocksLowerTriangular" | custom-call | tf_op jit(solution)/shard_map/jit(cholesky)/cholesky | solution.py:53
  152.3 25.1 %custom-call.60 = f32[2,128,128]{2,1,0:T(8,128)} custom-call(f32[2,128,128]{2,1,0:T(8,128)} %cholesky.538), custom_call_target="Cholesky" | custom-call | tf_op jit(solution)/shard_map/jit(cholesky)/cholesky | solution.py:53
  178.3 19.7 %custom-call.61 = f32[2,1,128,128]{2,3,1,0:T(8,128)S(1)} custom-call(f32[2,1,128,128]{3,2,1,0:T(8,128)S(1)} %get-tuple-element.192), custom_call_target="InvertDiagBlocksLowerTriangular" | custom-call | tf_op jit(solution)/shard_map/jit(cholesky)/cholesky | solution.py:53
  200.0 23.5 %custom-call.62 = f32[2,128,128]{2,1,0:T(8,128)S(1)} custom-call(f32[2,128,128]{2,1,0:T(8,128)S(1)} %cholesky.543), custom_call_target="Cholesky" | custom-call | tf_op jit(solution)/shard_map/jit(cholesky)/cholesky | solution.py:53
  223.5 20.8 %custom-call.63 = f32[2,1,128,128]{2,3,1,0:T(8,128)} custom-call(f32[2,1,128,128]{3,2,1,0:T(8,128)S(1)} %get-tuple-element.190), custom_call_target="InvertDiagBlocksLowerTriangular" | custom-call | tf_op jit(solution)/shard_map/jit(cholesky)/cholesky | solution.py:53
  246.9 23.5 %custom-call.64 = f32[2,128,128]{2,1,0:T(8,128)S(1)} custom-call(f32[2,128,128]{2,1,0:T(8,128)S(1)} %convolution_subtract_fusion.4), custom_call_target="Cholesky" | custom-call | tf_op jit(solution)/shard_map/jit(cholesky)/cholesky | solution.py:53
  274.3 2.5 collective-permute-start
  278.7 2.4 collective-permute-start.2
  281.1 3.4 collective-permute-start.3
  292.9 10.0 %conditional.18 = (f32[512,512]{1,0:T(8,128)S(1)}) conditional(s32[]{:T(128)} %convert_element_type.31, f32[512,512]{1,0:T(8,128)S(1)} %get-tuple-element.229, (s32[]{:T(128)}, s32[128,256]{1,0:T(8,128)}, f32[2,64,256]{1,2,0:T(8,128)S(1)}, f32[512,512]{1,0:T(8,128)S(1)}) %tuple.77), branch_computations={%region_33.34_spmd, %region_34.36_spmd} | conditional | flops 201589504 | bytes 2492466 | solution.py:27
  304.2 2.4 add.296
  308.7 57.5 %all-reduce.7.cloned.1.call-done = f32[512,512]{0,1:T(8,128)} async-done(((f32[512,512]{0,1:T(8,128)}), f32[512,512]{0,1:T(8,128)}) %all-reduce.7.cloned.1.call-update) | async-done | bytes 1048592 | tf_op jit(solution)/shard_map/psum | solution.py:73
  369.2 11.7 %cholesky.469 = f32[128,128]{1,0:T(8,128)S(1)} custom-call(f32[128,128]{1,0:T(8,128)S(1)} %cholesky.547), custom_call_target="Cholesky" | custom-call | tf_op jit(solution)/shard_map/jit(cholesky)/cholesky | solution.py:74
  381.0 9.8 %custom-call.65 = f32[1,128,128]{1,2,0:T(8,128)S(1)} custom-call(f32[1,128,128]{2,1,0:T(8,128)S(1)} %get-tuple-element.203), custom_call_target="InvertDiagBlocksLowerTriangular" | custom-call | tf_op jit(solution)/shard_map/jit(cholesky)/cholesky | solution.py:74
  393.4 11.7 %cholesky.485 = f32[128,128]{1,0:T(8,128)S(1)} custom-call(f32[128,128]{1,0:T(8,128)S(1)} %cholesky.551), custom_call_target="Cholesky" | custom-call | tf_op jit(solution)/shard_map/jit(cholesky)/cholesky | solution.py:74
  406.5 9.9 %custom-call.66 = f32[1,128,128]{1,2,0:T(8,128)S(1)} custom-call(f32[1,128,128]{2,1,0:T(8,128)S(1)} %get-tuple-element.200), custom_call_target="InvertDiagBlocksLowerTriangular" | custom-call | tf_op jit(solution)/shard_map/jit(cholesky)/cholesky | solution.py:74
  418.0 11.7 %cholesky.506 = f32[128,128]{1,0:T(8,128)S(1)} custom-call(f32[128,128]{1,0:T(8,128)S(1)} %cholesky.556), custom_call_target="Cholesky" | custom-call | tf_op jit(solution)/shard_map/jit(cholesky)/cholesky | solution.py:74
  430.4 9.8 %custom-call.67 = f32[1,128,128]{1,2,0:T(8,128)S(1)} custom-call(f32[1,128,128]{2,1,0:T(8,128)S(1)} %get-tuple-element.197), custom_call_target="InvertDiagBlocksLowerTriangular" | custom-call | tf_op jit(solution)/shard_map/jit(cholesky)/cholesky | solution.py:74
  441.7 11.7 %cholesky.523 = f32[128,128]{1,0:T(8,128)S(1)} custom-call(f32[128,128]{1,0:T(8,128)S(1)} %convolution_subtract_fusion.5), custom_call_target="Cholesky" | custom-call | tf_op jit(solution)/shard_map/jit(cholesky)/cholesky | solution.py:74
  (94 shorter events, 43.1 us)
Async XLA Ops:
  7.2 277.3 %copy-start = (f32[1,256,512]{2,1,0:T(8,128)S(1)}, f32[1,256,512]{2,1,0:T(8,128)}, u32[]{:S(2)}) copy-start(f32[1,256,512]{2,1,0:T(8,128)} %param.29) | copy-start | bytes 1572868
  7.2 90.8 %all-reduce.5.cloned.1.call-start = ((), (), s32[]{:S(2)}) async-start(), calls=%async_computation | async-start | bytes 4194304 | tf_op jit(solution)/shard_map/psum | solution.py:52
  31.1 335.2 %all-reduce.7.cloned.1.call-start = ((), (), s32[]{:S(2)}) async-start(), calls=%async_computation.1 | async-start | bytes 2097152 | tf_op jit(solution)/shard_map/psum | solution.py:73
  98.0 3.0 copy-start.1
  103.1 1.4 copy-start.3
  198.0 73.7 %copy-start.6 = (pred[512,512]{1,0:T(8,128)(4,1)S(1)}, pred[512,512]{1,0:T(8,128)(4,1)}, u32[]{:S(2)}) copy-start(pred[512,512]{1,0:T(8,128)(4,1)} %iota_compare_fusion) | copy-start | bytes 786436
  272.1 1.4 copy-start.2
  273.4 12.2 %copy-start.7 = (s32[128]{0:T(128)S(1)}, s32[128]{0:T(128)}, u32[]{:S(2)}) copy-start(s32[128]{0:T(128)} %param.27) | copy-start | bytes 1540
  274.3 18.5 %collective-permute-start = (f32[2,64,256]{1,2,0:T(8,128)}, f32[2,64,256]{1,2,0:T(8,128)}, u32[]{:S(2)}, u32[]{:S(2)}) collective-permute-start(f32[2,64,256]{1,2,0:T(8,128)} %constant_dynamic-slice_fusion), channel_id=1, source_target_pairs={{8,0},{12,4},{16,8},{20,12},{24,16},{28,20},{32,24},{36,28},{40,32... | collective-permute-start | bytes 393224 | tf_op jit(solution)/shard_map/ppermute | solution.py:16
  276.8 16.1 %collective-permute-start.1 = (f32[2,64,256]{1,2,0:T(8,128)}, f32[2,64,256]{1,2,0:T(8,128)}, u32[]{:S(2)}, u32[]{:S(2)}) collective-permute-start(f32[2,64,256]{1,2,0:T(8,128)} %constant_dynamic-slice_fusion), channel_id=1, source_target_pairs={{4,0},{8,4},{12,8},{16,12},{20,16},{24,20},{28,24},{32,28},{36,32}... | collective-permute-start | bytes 393224 | tf_op jit(solution)/shard_map/ppermute | solution.py:16
  278.7 14.2 %collective-permute-start.2 = (f32[2,64,256]{1,2,0:T(8,128)}, f32[2,64,256]{1,2,0:T(8,128)S(1)}, u32[]{:S(2)}, u32[]{:S(2)}) collective-permute-start(f32[2,64,256]{1,2,0:T(8,128)} %constant_dynamic-slice_fusion), channel_id=1, source_target_pairs={{0,4},{4,8},{8,12},{12,16},{16,20},{20,24},{24,28},{28,32},{32,36}... | collective-permute-start | bytes 393224 | tf_op jit(solution)/shard_map/ppermute | solution.py:16
  281.1 11.8 %collective-permute-start.3 = (f32[2,64,256]{1,2,0:T(8,128)}, f32[2,64,256]{1,2,0:T(8,128)S(1)}, u32[]{:S(2)}, u32[]{:S(2)}) collective-permute-start(f32[2,64,256]{1,2,0:T(8,128)} %constant_dynamic-slice_fusion), channel_id=1, source_target_pairs={{0,8},{4,12},{8,16},{12,20},{16,24},{20,28},{24,32},{28,36},{32,40... | collective-permute-start | bytes 393224 | tf_op jit(solution)/shard_map/ppermute | solution.py:16
  306.6 1.2 slice-start
  366.3 1.7 copy-start.4
  368.2 1.0 copy-start.5
Sparse Core Ops, SparseCore 0:
  31.2 66.7 all-reduce.4
  306.8 59.4 all-reduce.6
where the time goes:
time: 473 us; the launch traced here: 465 us
  other arithmetic  246 us (52%)
  waiting for transfers between devices  123 us (26%)
  matrix products  38.9 us (8%)
  between operations  23.5 us (5%)
  local copies, waits for them, and re-layouts  16.8 us (4%)
  starting transfers between devices  10.4 us (2%)
  loops' own time  7.06 us (1%)
    another operation x16, other arithmetic, per_device(): upper = jnp.swapaxes(jnp.linalg.cholesky(leaf_gram), 1, 2)  158 us
    another operation x15, other arithmetic, per_device(): parent_upper = jnp.linalg.cholesky(parent_gram).T  79.3 us
    psum x1, waiting for transfers between devices, per_device(): leaf_gram = lax.psum(local_gram, 'row')  65.3 us
    psum x1, waiting for transfers between devices, per_device(): parent_gram = lax.psum(own_gram + children, 'row')  57.5 us
    dot_general x1, matrix products, per_device(): jnp.einsum('kra,krb->kab', masked, masked, precision=HIGHEST) / total_rows  23 us
    ppermute x4, starting transfers between devices, passed_along(): lax.ppermute(value, axis, [(source, source + steps) for source in range(i...  10.2 us
  transfers between devices with their start and end apart: 6, of which 2 were waited for; matrix products, arithmetic and copies ran while one was open for 1% of the time, Pallas kernels for 0%

commit v1 on v0

v1 whole, which is shorter than its diff:
```python
import jax
import jax.numpy as jnp
from jax import lax
from jax.experimental import pallas as pl
from jax.experimental.pallas import tpu as pltpu
from jax.sharding import PartitionSpec as P

F32, BF16 = jnp.float32, jnp.bfloat16
MESH = pl.DeviceIdType.MESH
N = 512
H = 128
BLOCKS = [(i, j) for i in range(4) for j in range(i, 4)]
CHUNKS = ((0, 1), (1, 4), (4, 7), (7, 10))
REACH = 2


def split(x):
    high = x.astype(BF16)
    return high, (x - high.astype(F32)).astype(BF16)


def nn(a, b):
    return jnp.dot(a, b, preferred_element_type=F32)


def tn(a, b):
    return lax.dot_general(a, b, (((0,), (0,)), ((), ())), preferred_element_type=F32)


def nt(a, b):
    return lax.dot_general(a, b, (((1,), (1,)), ((), ())), preferred_element_type=F32)


def nn3(a, b):
    ah, al = split(a)
    bh, bl = split(b)
    return nn(ah, bh) + (nn(ah, bl) + nn(al, bh))


def spread_row(x, p):
    return jnp.broadcast_to(x[p : p + 1, :], (8, H))


def spread_column(x, k):
    return jnp.broadcast_to(x[:, k : k + 1], (8, H))


def tree(terms):
    while len(terms) > 1:
        terms = [terms[i] + terms[i + 1] for i in range(0, len(terms), 2)]
    return terms[0]


def factor_block(a):
    sub = lax.broadcasted_iota(jnp.int32, (8, H), 0)
    lane = lax.broadcasted_iota(jnp.int32, (8, H), 1)
    count = H // 8
    tiles = [[a[8 * t : 8 * t + 8, :], (lane == sub + 8 * t).astype(F32)] for t in range(count)]
    factor, inverse = [], []
    for t in range(count):
        j = 8 * t
        left, right = tiles[t]
        column = [spread_column(left, j + k) for k in range(8)]
        if t + 1 < count:
            following = [spread_column(tiles[t + 1][0], j + k) for k in range(8)]
        frow = jnp.zeros((8, H), F32)
        irow = jnp.zeros((8, H), F32)
        for p in range(8):
            here = sub == p
            pivot = spread_row(column[p], p)
            inv = 1.0 / pivot
            root = lax.rsqrt(pivot)

            def eliminate(z):
                row = spread_row(z, p)
                return jnp.where(here, row * inv, z - (column[p] * row) * inv)

            frow = jnp.where(here, left * root, frow)
            irow = jnp.where(here, right * root, irow)
            for k in range(p + 1, 8):
                column[k] = eliminate(column[k])
            left, right = eliminate(left), eliminate(right)
        factor.append(jnp.where(lane >= sub + j, frow, 0.0))
        inverse.append(irow)
        if t + 1 < count:
            nxt = [
                old - tree([following[p] * spread_row(new, p) for p in range(8)])
                for old, new in zip(tiles[t + 1], (left, right))
            ]
            if t + 2 < count:
                below = jnp.concatenate([tiles[u][0] for u in range(t + 2, count)], 0)
                parts = [jnp.concatenate([left, right], 1)]
                if j:
                    parts = [jnp.zeros((j, 2 * H), F32)] + parts
                parts.append(jnp.zeros((H - 8 - j, 2 * H), F32))
                change = nn3(below, jnp.concatenate(parts, 0))
                for u in range(t + 2, count):
                    rows = change[8 * (u - t - 2) : 8 * (u - t - 1)]
                    tiles[u] = [tiles[u][0] - rows[:, :H], tiles[u][1] - rows[:, H:]]
            tiles[t + 1] = nxt
    return jnp.concatenate(factor, 0), jnp.concatenate(inverse, 0)


def kernel(
    rows_ref, parent_ref, map_ref, leaf_hbm, prow_hbm, lf_out, pf_out,
    xs, ps, hh, hl, gram, far, near, work, fac, fac_h, fac_l, rleaf, rpar, slots,
    load_sem, far_send, far_recv, near_send, near_recv, lf_send, lf_recv, slot_send, slot_recv, pf_send, pf_recv,
):
    r = lax.axis_index("row")
    l = lax.axis_index("leaf")
    leaves = lax.axis_size("leaf")
    core = lax.rem(l, 2)
    live_rows = xs.shape[1]
    pieces = load_sem.shape[1]
    piece = live_rows // pieces

    def mod4(v):
        return lax.rem(v + 8, 4)

    place = [mod4(r - (2 * core + k)) for k in range(2)]
    first = jnp.where(jnp.logical_or(place[0] == 0, place[0] == 3), 1, 0)
    rp = 3 - 2 * core
    place.append(mod4(r - rp))

    def load(step, c):
        k = first if step == 0 else 1 - first
        part = pl.ds(c * piece, piece)
        return pltpu.make_async_copy(leaf_hbm.at[k, part], xs.at[k, part], load_sem.at[step, c])

    for step in range(2):
        for c in range(pieces):
            load(step, c).start()
    prow_copy = pltpu.make_async_copy(prow_hbm.at[0], ps, load_sem.at[2, 0])
    prow_copy.start()

    barrier = pltpu.get_barrier_semaphore()
    for step in (1, 2, 3):
        pl.semaphore_signal(barrier, inc=1, device_id={"row": mod4(r + step)}, device_id_type=MESH)
    greeted = 3
    for delta in (-2, -1, 1, 2):
        inside = jnp.logical_and(l + delta >= 0, l + delta < leaves)

        @pl.when(inside)
        def _(delta=delta):
            pl.semaphore_signal(barrier, inc=1, device_id={"leaf": l + delta}, device_id_type=MESH)

        greeted = greeted + jnp.where(inside, 1, 0)
    pl.semaphore_wait(barrier, greeted)

    def far_copy(u, ci, side):
        b0, b1 = CHUNKS[ci]
        return pltpu.make_async_remote_copy(
            src_ref=gram.at[u, b0:b1, pl.ds(64 * side, 64)],
            dst_ref=far.at[u, b0:b1],
            send_sem=far_send.at[u, side, ci],
            recv_sem=far_recv.at[u, ci],
            device_id={"row": mod4(r - 1 + 2 * side)},
            device_id_type=MESH,
        )

    def near_copy(u, ci, side):
        b0, b1 = CHUNKS[ci]
        return pltpu.make_async_remote_copy(
            src_ref=gram.at[u, b0:b1],
            dst_ref=near.at[u, side, b0:b1],
            send_sem=near_send.at[u, ci],
            recv_sem=near_recv.at[u, side, ci],
            device_id={"row": mod4(r - 1 + 2 * side)},
            device_id_type=MESH,
        )

    def start_far(u):
        @pl.when(place[u] == 2)
        def _():
            for ci in range(len(CHUNKS)):
                for side in range(2):
                    far_copy(u, ci, side).start()

    def forward(u):
        for side in range(2):

            @pl.when(place[u] == 1 + 2 * side)
            def _(side=side):
                for ci, (b0, b1) in enumerate(CHUNKS):
                    far_copy(u, ci, side).wait_recv()
                    half = pl.ds(64 * side, 64)
                    gram[u, b0:b1, half] = gram[u, b0:b1, half] + far[u, b0:b1]
                    near_copy(u, ci, side).start()

    def wait_near(u, ci):
        for side in range(2):
            near_copy(u, ci, side).wait_recv()

    def drain(u):
        @pl.when(place[u] == 2)
        def _():
            for ci in range(len(CHUNKS)):
                for side in range(2):
                    far_copy(u, ci, side).wait_send()

        for side in range(2):

            @pl.when(place[u] == 1 + 2 * side)
            def _(side=side):
                for ci in range(len(CHUNKS)):
                    near_copy(u, ci, side).wait_send()

    def summed(u, b):
        return gram[u, b] + (near[u, 0, b] + near[u, 1, b])

    def add_gram(x, start):
        high, low = split(x)
        for ref, rows, columns, other in (
            (hh, slice(0, 256), slice(0, N), high),
            (hh, slice(256, N), slice(256, N), high),
            (hl, slice(0, N), slice(0, N), low),
        ):
            value = tn(high[:, rows], other[:, columns])
            ref[rows, columns] = value if start else ref[rows, columns] + value

    def finish_gram(u, scale):
        for b, (i, j) in enumerate(BLOCKS):
            rows, columns = slice(H * i, H * i + H), slice(H * j, H * j + H)
            gram[u, b] = (hh[rows, columns] + (hl[rows, columns] + hl[columns, rows].T)) * scale

    total = 4 * live_rows
    for step in range(2):
        k = first if step == 0 else 1 - first
        live = rows_ref[k] - r * live_rows
        for c in range(pieces):
            load(step, c).wait()
            x = xs[k, pl.ds(c * piece, piece)]
            position = lax.broadcasted_iota(jnp.int32, (piece, N), 0) + c * piece
            add_gram(jnp.where(position < live, x, 0.0), c == 0)
        finish_gram(k, 1.0 / total)
        if step == 0:
            start_far(0)
            start_far(1)
    forward(0)
    forward(1)
    prow_copy.wait()
    add_gram(ps[...], True)
    finish_gram(2, 1.0 / (4 * ps.shape[0]))

    block_of = lax.broadcasted_iota(jnp.int32, (H, N), 1) // H

    def factor_rows(b, out):
        columns = pl.ds(pl.multiple_of(b * H, H), H)

        @pl.when(b > 0)
        def _():
            high, low = fac_h[:, columns], fac_l[:, columns]
            whole_h, whole_l = fac_h[...], fac_l[...]
            work[b] = work[b] - (tn(high, whole_h) + (tn(high, whole_l) + tn(low, whole_h)))

        diagonal, inverse = factor_block(work[b, :, columns])
        panel = jnp.where(block_of > b, nn3(inverse, work[b]), 0.0)
        fac[...] = panel
        fac[:, columns] = diagonal
        here = pl.ds(pl.multiple_of(b * H, H), H)
        fac_h[here], fac_l[here] = split(fac[...])
        for q in range(4):
            out[b, q] = fac[:, q * H : q * H + H]

    def fill_rows(u, ci):
        wait_near(u, ci)
        b0, b1 = CHUNKS[ci]
        for b in range(b0, b1):
            i, j = BLOCKS[b]
            work[i, :, j * H : j * H + H] = summed(u, b)

    k_mine = r - 2 * core
    factors = jnp.logical_and(k_mine >= 0, k_mine < 2)

    def lf_copy(k, b, q):
        return pltpu.make_async_remote_copy(
            src_ref=rleaf.at[b, q],
            dst_ref=lf_out.at[k, b * H : b * H + H],
            send_sem=lf_send.at[b, q],
            recv_sem=lf_recv.at[k, b],
            device_id={"row": q},
            device_id_type=MESH,
        )

    def slot_copy(delta):
        return pltpu.make_async_remote_copy(
            src_ref=slots.at[2],
            dst_ref=slots.at[2 + delta],
            send_sem=slot_send.at[2 + delta],
            recv_sem=slot_recv.at[2 + delta],
            device_id={"leaf": l + delta},
            device_id_type=MESH,
        )

    work[...] = jnp.zeros_like(work)
    fac_h[...] = jnp.zeros_like(fac_h)
    fac_l[...] = jnp.zeros_like(fac_l)

    @pl.when(factors)
    def _():
        def step(b, carry):
            @pl.when(b == 0)
            def _():
                for k in range(2):

                    @pl.when(k_mine == k)
                    def _(k=k):
                        fill_rows(k, 0)
                        fill_rows(k, 1)

            @pl.when(b == 1)
            def _():
                for k in range(2):

                    @pl.when(k_mine == k)
                    def _(k=k):
                        fill_rows(k, 2)

            factor_rows(b, rleaf)
            for q in range(4):

                @pl.when(jnp.logical_and(q != r, q >= b))
                def _(q=q):
                    for k in range(2):
                        for bb in range(2):

                            @pl.when(jnp.logical_and(k_mine == k, b == bb))
                            def _(k=k, bb=bb):
                                lf_copy(k, bb, q).start()

            return carry

        lax.fori_loop(0, 2, step, 0)
        for k in range(2):

            @pl.when(k_mine == k)
            def _(k=k):
                wait_near(k, 3)
                for b in range(2):

                    for q in range(4):

                        @pl.when(jnp.logical_and(q == r, q >= b))
                        def _(q=q, b=b):
                            lf_out[k, b * H : b * H + H] = rleaf[b, q]

        for i in range(2):
            rows = slice(256 + H * i, 384 + H * i)
            columns = slice(256 + H * i, N)
            left_h, left_l = fac_h[0:256, rows], fac_l[0:256, rows]
            right_h, right_l = fac_h[0:256, columns], fac_l[0:256, columns]
            taken = tn(left_h, right_h) + (tn(left_h, right_l) + tn(left_l, right_h))
            for j in range(i, 2):
                b = 7 + i + j
                slots[2, i + j] = summed(k_mine, b) - taken[:, (j - i) * H : (j - i) * H + H]
        for delta in (-2, -1, 1, 2):

            @pl.when(jnp.logical_and(l + delta >= 0, l + delta < leaves))
            def _(delta=delta):
                slot_copy(delta).start()

    for k in range(2):

        @pl.when(r == 0)
        def _(k=k):
            lf_out[k, H : 2 * H] = jnp.zeros((H, H), F32)

    for b in range(1, 4):

        @pl.when(b > r)
        def _(b=b):
            pf_out[0, b * H : b * H + H] = jnp.zeros((H, H), F32)

    even = lax.rem(l, 2) == r // 2

    for delta in range(-REACH, REACH + 1):
        source = l - delta
        parity = even if delta % 2 == 0 else jnp.logical_not(even)
        valid = jnp.logical_and(parity, jnp.logical_and(source >= 0, source < leaves))

        @pl.when(valid)
        def _(delta=delta, source=source):
            if delta != 0:
                slot_copy(delta).wait_recv()
            front = 2 * source + lax.rem(r, 2)
            away = jnp.where(parent_ref[front] == l, 0, 2 * N)
            target = map_ref[pl.ds(front, 1), :] + away
            chosen = (lax.broadcasted_iota(jnp.int32, (N, 256), 0) == target).astype(F32).astype(BF16)
            s = slots[2 + delta]
            square = jnp.concatenate(
                [jnp.concatenate([s[0], s[1]], 1), jnp.concatenate([s[1].T, s[2]], 1)], 0
            )
            high, low = split(square)
            high_rows, low_rows = nn(chosen, high).astype(BF16), nn(chosen, low).astype(BF16)
            for half in range(2):
                rows, columns = slice(256 * half, 256 * half + 256), slice(256 * half, N)
                placed = nt(high_rows[rows], chosen[columns]) + nt(low_rows[rows], chosen[columns])
                for b, (i, j) in enumerate(BLOCKS):
                    if i // 2 == half:
                        ii, jj = (i - 2 * half) * H, (j - 2 * half) * H
                        gram[2, b] = gram[2, b] + placed[ii : ii + H, jj : jj + H]

    start_far(2)
    forward(2)

    def pf_copy(b, q):
        return pltpu.make_async_remote_copy(
            src_ref=rpar.at[b, q],
            dst_ref=pf_out.at[0, b * H : b * H + H],
            send_sem=pf_send.at[b, q],
            recv_sem=pf_recv.at[b],
            device_id={"row": q},
            device_id_type=MESH,
        )

    @pl.when(place[2] == 0)
    def _():
        fac_h[...] = jnp.zeros_like(fac_h)
        fac_l[...] = jnp.zeros_like(fac_l)

        def step(b, carry):
            for ci in range(1, 4):

                @pl.when(b == ci - 1)
                def _(ci=ci):
                    if ci == 1:
                        fill_rows(2, 0)
                    fill_rows(2, ci)
            @pl.when(b == 2)
            def _():
                pass

            factor_rows(b, rpar)
            for q in range(4):
                for bb in range(q + 1):

                    @pl.when(jnp.logical_and(q != r, b == bb))
                    def _(q=q, bb=bb):
                        pf_copy(bb, q).start()

                    @pl.when(jnp.logical_and(q == r, b == bb))
                    def _(q=q, bb=bb):
                        pf_out[0, bb * H : bb * H + H] = rpar[bb, q]

            return carry

        lax.fori_loop(0, 4, step, 0)
        for q in range(4):

            @pl.when(q != r)
            def _(q=q):
                for bb in range(q + 1):
                    pf_copy(bb, q).wait_send()

    @pl.when(place[2] != 0)
    def _():
        for bb in range(4):

            @pl.when(bb <= r)
            def _(bb=bb):
                pf_copy(bb, 0).wait_recv()

    for k in range(2):

        @pl.when(k_mine != k)
        def _(k=k):
            lf_copy(k, 0, 0).wait_recv()

            @pl.when(r > 0)
            def _():
                lf_copy(k, 1, 0).wait_recv()

        @pl.when(k_mine == k)
        def _(k=k):
            for q in range(4):

                @pl.when(q != r)
                def _(q=q):
                    for b in range(min(q, 1) + 1):
                        lf_copy(k, b, q).wait_send()

    @pl.when(factors)
    def _():
        for delta in (-2, -1, 1, 2):

            @pl.when(jnp.logical_and(l + delta >= 0, l + delta < leaves))
            def _(delta=delta):
                slot_copy(delta).wait_send()

    for u in range(3):
        drain(u)


def per_device(leaf_fronts, front_rows, parent_of, column_map, parent_rows):
    kids, live_rows, _ = leaf_fronts.shape
    chunks = len(CHUNKS)
    dma = pltpu.SemaphoreType.DMA
    vmem = pltpu.VMEM
    return pl.pallas_call(
        kernel,
        out_shape=(
            jax.ShapeDtypeStruct((kids, 256, H), F32),
            jax.ShapeDtypeStruct((1, N, H), F32),
        ),
        in_specs=[
            pl.BlockSpec(memory_space=pltpu.SMEM),
            pl.BlockSpec(memory_space=pltpu.SMEM),
            pl.BlockSpec(memory_space=pltpu.VMEM),
            pl.BlockSpec(memory_space=pl.ANY),
            pl.BlockSpec(memory_space=pl.ANY),
        ],
        out_specs=(pl.BlockSpec(memory_space=pltpu.VMEM),) * 2,
        scratch_shapes=[
            vmem((kids, live_rows, N), F32),
            vmem(parent_rows.shape[1:], F32),
            vmem((N, N), F32),
            vmem((N, N), F32),
            vmem((3, 10, H, H), F32),
            vmem((3, 10, H // 2, H), F32),
            vmem((3, 2, 10, H, H), F32),
            vmem((4, H, N), F32),
            vmem((H, N), F32),
            vmem((N, N), BF16),
            vmem((N, N), BF16),
            vmem((2, 4, H, H), F32),
            vmem((4, 4, H, H), F32),
            vmem((5, 3, H, H), F32),
            dma((3, 2)),
            dma((3, 2, chunks)),
            dma((3, chunks)),
            dma((3, chunks)),
            dma((3, 2, chunks)),
            dma((2, 4)),
            dma((2, 2)),
            dma((5,)),
            dma((5,)),
            dma((4, 4)),
            dma((4,)),
        ],
        compiler_params=pltpu.CompilerParams(
            collective_id=0, has_side_effects=True, vmem_limit_bytes=48 << 20
        ),
        name="fronts",
    )(front_rows, parent_of, column_map, leaf_fronts, parent_rows)


def solution(mesh):
    return jax.shard_map(
        per_device,
        mesh=mesh,
        in_specs=(P("leaf", "row", None), P("leaf"), P(), P(), P("leaf", "row", None)),
        out_specs=(P("leaf", None, "row"), P("leaf", None, "row")),
        check_vma=False,
    )
```

time: 473 us -> 65.5 us (0.14)
  the two profiles are of different devices: /device:TPU:2 before, /device:TPU:153 now
where the time goes in v1:
time: 65.5 us; the launch traced here: 65.3 us
  Pallas kernels  60 us (92%)
  local copies, waits for them, and re-layouts  4.66 us (7%)
    pallas_call x1, Pallas kernels, per_device(): pl.pallas_call(kernel, out_shape=(jax.ShapeDtypeStruct((kids, 256, H), F3...  60 us
    unnamed x10, local copies, waits for them, and re-layouts  4.66 us

profile of v1, /device:TPU:153, one launch (start us, length us, event | category | flops | bytes accessed | tf_op | source)
XLA Modules:
  0.0 65.3 jit_solution(5507291361808253370)
XLA Ops:
  0.6 0.0 copy-start
  0.6 1.0 %copy-done = f32[1,256,512]{2,1,0:T(8,128)S(1)} copy-done((f32[1,256,512]{2,1,0:T(8,128)S(1)}, f32[1,256,512]{2,1,0:T(8,128)}, u32[]{:S(2)}) %copy-start) | copy-done | bytes 524312
  1.7 0.0 copy-start.1
  1.7 0.9 %copy-done.1 = s32[128,256]{1,0:T(8,128)S(1)} copy-done((s32[128,256]{1,0:T(8,128)S(1)}, s32[128,256]{1,0:T(8,128)}, u32[]{:S(2)}) %copy-start.1) | copy-done | bytes 131096
  2.6 0.0 copy-start.2
  2.6 0.7 %copy-done.2 = s32[2]{0:T(128)S(1)} copy-done((s32[2]{0:T(128)S(1)}, s32[2]{0:T(128)}, u32[]{:S(2)}) %copy-start.2) | copy-done | bytes 32
  3.2 0.0 copy-start.3
  3.2 0.7 %copy-done.3 = s32[128]{0:T(128)S(1)} copy-done((s32[128]{0:T(128)S(1)}, s32[128]{0:T(128)}, u32[]{:S(2)}) %copy-start.3) | copy-done | bytes 536
  3.9 60.0 %fronts.1 = (f32[2,256,128]{2,1,0:T(8,128)S(1)}, f32[1,512,128]{2,1,0:T(8,128)S(1)}) custom-call(s32[2]{0:T(128)S(1)} %copy-done.2, s32[128]{0:T(128)S(1)} %copy-done.3, s32[128,256]{1,0:T(8,128)S(1)} %copy-done.1, f32[2,2048,512]{2,1,0:T(8,128)} %leaf_hbm.1, f32[1,256,512]{2,1,0:T(8,128)S(1)} %copy-done), custom_call_target="tpu_custom_call" | custom-call | tf_op jit(solution)/shard_map/fronts/pallas_call | solution.py:499
  63.9 0.7 %copy.9 = f32[2,256,128]{2,1,0:T(8,128)} copy(f32[2,256,128]{2,1,0:T(8,128)S(1)} %get-tuple-element.4) | data formatting | bytes 524288
  64.6 0.7 %copy.10 = f32[1,512,128]{2,1,0:T(8,128)} copy(f32[1,512,128]{2,1,0:T(8,128)S(1)} %get-tuple-element.5) | data formatting | bytes 524288
Async XLA Ops:
  0.6 1.0 %copy-start = (f32[1,256,512]{2,1,0:T(8,128)S(1)}, f32[1,256,512]{2,1,0:T(8,128)}, u32[]{:S(2)}) copy-start(f32[1,256,512]{2,1,0:T(8,128)} %prow_hbm.1) | copy-start | bytes 1572868
  1.7 0.9 %copy-start.1 = (s32[128,256]{1,0:T(8,128)S(1)}, s32[128,256]{1,0:T(8,128)}, u32[]{:S(2)}) copy-start(s32[128,256]{1,0:T(8,128)} %map_ref.1) | copy-start | bytes 393220
  2.6 0.7 %copy-start.2 = (s32[2]{0:T(128)S(1)}, s32[2]{0:T(128)}, u32[]{:S(2)}) copy-start(s32[2]{0:T(128)} %rows_ref.1) | copy-start | bytes 28
  3.2 0.7 %copy-start.3 = (s32[128]{0:T(128)S(1)}, s32[128]{0:T(128)}, u32[]{:S(2)}) copy-start(s32[128]{0:T(128)} %parent_ref.1) | copy-start | bytes 1540

commit v2 on v1

--- a/solution.py
+++ b/solution.py
@@ -10,7 +10,7 @@
 N = 512
 H = 128
 BLOCKS = [(i, j) for i in range(4) for j in range(i, 4)]
-CHUNKS = ((0, 1), (1, 4), (4, 7), (7, 10))
+CHUNKS = ((1, 4), (4, 7), (7, 10))
 REACH = 2
 
 
@@ -37,12 +37,22 @@
     return nn(ah, bh) + (nn(ah, bl) + nn(al, bh))
 
 
+def nn3_stacked(a, b):
+    ah, al = split(a)
+    bh, bl = split(b)
+    return nn(jnp.concatenate([ah, al, ah], 1), jnp.concatenate([bh, bh, bl], 0))
+
+
+def tn3(ah, al, bh, bl):
+    return tn(ah, bh) + (tn(ah, bl) + tn(al, bh))
+
+
 def spread_row(x, p):
     return jnp.broadcast_to(x[p : p + 1, :], (8, H))
 
 
 def spread_column(x, k):
-    return jnp.broadcast_to(x[:, k : k + 1], (8, H))
+    return jnp.take_along_axis(x, jnp.full((8, H), k, jnp.int32), axis=1)
 
 
 def tree(terms):
@@ -71,9 +81,10 @@
             inv = 1.0 / pivot
             root = lax.rsqrt(pivot)
 
+            signed = jnp.where(here, -1.0, column[p])
+
             def eliminate(z):
-                row = spread_row(z, p)
-                return jnp.where(here, row * inv, z - (column[p] * row) * inv)
+                return jnp.where(here, 0.0, z) - (signed * spread_row(z, p)) * inv
 
             frow = jnp.where(here, left * root, frow)
             irow = jnp.where(here, right * root, irow)
@@ -93,7 +104,7 @@
                 if j:
                     parts = [jnp.zeros((j, 2 * H), F32)] + parts
                 parts.append(jnp.zeros((H - 8 - j, 2 * H), F32))
-                change = nn3(below, jnp.concatenate(parts, 0))
+                change = nn3_stacked(below, jnp.concatenate(parts, 0))
                 for u in range(t + 2, count):
                     rows = change[8 * (u - t - 2) : 8 * (u - t - 1)]
                     tiles[u] = [tiles[u][0] - rows[:, :H], tiles[u][1] - rows[:, H:]]
@@ -102,9 +113,11 @@
 
 
 def kernel(
-    rows_ref, parent_ref, map_ref, leaf_hbm, prow_hbm, lf_out, pf_out,
-    xs, ps, hh, hl, gram, far, near, work, fac, fac_h, fac_l, rleaf, rpar, slots,
-    load_sem, far_send, far_recv, near_send, near_recv, lf_send, lf_recv, slot_send, slot_recv, pf_send, pf_recv,
+    rows_hbm, parent_hbm, map_hbm, leaf_hbm, prow_hbm, lf_out, pf_out,
+    rows_ref, parent_ref, map_ref, xs, ps, hh, hl, gram, far, near, direct,
+    work, diag, upd, fac, fac_h, fac_l, rleaf, rpar, slots,
+    load_sem, small_sem, direct_send, direct_recv, far_send, far_recv, near_send, near_recv,
+    lf_send, lf_recv, slot_send, slot_recv, pf_send, pf_recv,
 ):
     r = lax.axis_index("row")
     l = lax.axis_index("leaf")
@@ -121,17 +134,9 @@
     first = jnp.where(jnp.logical_or(place[0] == 0, place[0] == 3), 1, 0)
     rp = 3 - 2 * core
     place.append(mod4(r - rp))
-
-    def load(step, c):
-        k = first if step == 0 else 1 - first
-        part = pl.ds(c * piece, piece)
-        return pltpu.make_async_copy(leaf_hbm.at[k, part], xs.at[k, part], load_sem.at[step, c])
-
-    for step in range(2):
-        for c in range(pieces):
-            load(step, c).start()
-    prow_copy = pltpu.make_async_copy(prow_hbm.at[0], ps, load_sem.at[2, 0])
-    prow_copy.start()
+    k_mine = r - 2 * core
+    factors = jnp.logical_and(k_mine >= 0, k_mine < 2)
+    k_here = jnp.clip(k_mine, 0, 1)
 
     barrier = pltpu.get_barrier_semaphore()
     for step in (1, 2, 3):
@@ -145,7 +150,34 @@
             pl.semaphore_signal(barrier, inc=1, device_id={"leaf": l + delta}, device_id_type=MESH)
 
         greeted = greeted + jnp.where(inside, 1, 0)
-    pl.semaphore_wait(barrier, greeted)
+
+    def load(step, c):
+        k = first if step == 0 else 1 - first
+        part = pl.ds(c * piece, piece)
+        return pltpu.make_async_copy(leaf_hbm.at[k, part], xs.at[k, part], load_sem.at[step, c])
+
+    small = [
+        pltpu.make_async_copy(rows_hbm, rows_ref, small_sem.at[0]),
+        pltpu.make_async_copy(parent_hbm, parent_ref, small_sem.at[1]),
+        pltpu.make_async_copy(map_hbm, map_ref, small_sem.at[2]),
+        pltpu.make_async_copy(prow_hbm.at[0], ps, small_sem.at[3]),
+    ]
+    small[0].start()
+    for step in range(2):
+        for c in range(pieces):
+            load(step, c).start()
+    for copy in small[1:]:
+        copy.start()
+
+    def direct_copy(u):
+        return pltpu.make_async_remote_copy(
+            src_ref=gram.at[u, 0],
+            dst_ref=direct.at[u],
+            send_sem=direct_send.at[u],
+            recv_sem=direct_recv.at[u],
+            device_id={"row": mod4(r + 2)},
+            device_id_type=MESH,
+        )
 
     def far_copy(u, ci, side):
         b0, b1 = CHUNKS[ci]
@@ -159,22 +191,29 @@
         )
 
     def near_copy(u, ci, side):
-        b0, b1 = CHUNKS[ci]
+        b0, b1 = CHUNKS[ci] if ci >= 0 else (0, 1)
         return pltpu.make_async_remote_copy(
             src_ref=gram.at[u, b0:b1],
             dst_ref=near.at[u, side, b0:b1],
-            send_sem=near_send.at[u, ci],
-            recv_sem=near_recv.at[u, side, ci],
+            send_sem=near_send.at[u, ci + 1],
+            recv_sem=near_recv.at[u, side, ci + 1],
             device_id={"row": mod4(r - 1 + 2 * side)},
             device_id_type=MESH,
         )
 
-    def start_far(u):
+    def start_first(u):
         @pl.when(place[u] == 2)
         def _():
+            direct_copy(u).start()
             for ci in range(len(CHUNKS)):
                 for side in range(2):
                     far_copy(u, ci, side).start()
+
+        for side in range(2):
+
+            @pl.when(place[u] == 1 + 2 * side)
+            def _(side=side):
+                near_copy(u, -1, side).start()
 
     def forward(u):
         for side in range(2):
@@ -188,12 +227,15 @@
                     near_copy(u, ci, side).start()
 
     def wait_near(u, ci):
+        if ci < 0:
+            direct_copy(u).wait_recv()
         for side in range(2):
             near_copy(u, ci, side).wait_recv()
 
     def drain(u):
         @pl.when(place[u] == 2)
         def _():
+            direct_copy(u).wait_send()
             for ci in range(len(CHUNKS)):
                 for side in range(2):
                     far_copy(u, ci, side).wait_send()
@@ -202,7 +244,7 @@
 
             @pl.when(place[u] == 1 + 2 * side)
             def _(side=side):
-                for ci in range(len(CHUNKS)):
+                for ci in range(-1, len(CHUNKS)):
                     near_copy(u, ci, side).wait_send()
 
     def summed(u, b):
@@ -224,6 +266,7 @@
             gram[u, b] = (hh[rows, columns] + (hl[rows, columns] + hl[columns, rows].T)) * scale
 
     total = 4 * live_rows
+    small[0].wait()
     for step in range(2):
         k = first if step == 0 else 1 - first
         live = rows_ref[k] - r * live_rows
@@ -234,33 +277,17 @@
             add_gram(jnp.where(position < live, x, 0.0), c == 0)
         finish_gram(k, 1.0 / total)
         if step == 0:
-            start_far(0)
-            start_far(1)
+            pl.semaphore_wait(barrier, greeted)
+        for u in range(2):
+
+            @pl.when(k == u)
+            def _(u=u):
+                start_first(u)
+
     forward(0)
     forward(1)
-    prow_copy.wait()
-    add_gram(ps[...], True)
-    finish_gram(2, 1.0 / (4 * ps.shape[0]))
 
     block_of = lax.broadcasted_iota(jnp.int32, (H, N), 1) // H
-
-    def factor_rows(b, out):
-        columns = pl.ds(pl.multiple_of(b * H, H), H)
-
-        @pl.when(b > 0)
-        def _():
-            high, low = fac_h[:, columns], fac_l[:, columns]
-            whole_h, whole_l = fac_h[...], fac_l[...]
-            work[b] = work[b] - (tn(high, whole_h) + (tn(high, whole_l) + tn(low, whole_h)))
-
-        diagonal, inverse = factor_block(work[b, :, columns])
-        panel = jnp.where(block_of > b, nn3(inverse, work[b]), 0.0)
-        fac[...] = panel
-        fac[:, columns] = diagonal
-        here = pl.ds(pl.multiple_of(b * H, H), H)
-        fac_h[here], fac_l[here] = split(fac[...])
-        for q in range(4):
-            out[b, q] = fac[:, q * H : q * H + H]
 
     def fill_rows(u, ci):
         wait_near(u, ci)
@@ -269,13 +296,39 @@
             i, j = BLOCKS[b]
             work[i, :, j * H : j * H + H] = summed(u, b)
 
-    k_mine = r - 2 * core
-    factors = jnp.logical_and(k_mine >= 0, k_mine < 2)
+    def factor_rows(u, b, out):
+        columns = pl.ds(pl.multiple_of(b * H, H), H)
+        later = jnp.minimum(b + 1, 3)
+        ncolumns = pl.ds(pl.multiple_of(later * H, H), H)
+        whole_h, whole_l = fac_h[...], fac_l[...]
+        upd[:, 0:N] = tn3(fac_h[:, columns], fac_l[:, columns], whole_h, whole_l)
+        nh, nl = fac_h[:, ncolumns], fac_l[:, ncolumns]
+        upd[:, N : N + H] = tn3(nh, nl, nh, nl)
+        diagonal, inverse = factor_block(diag[...])
+
+        @pl.when(b == 0)
+        def _():
+            fill_rows(u, 0)
+            fill_rows(u, 1)
+
+        @pl.when(b == 1)
+        def _():
+            fill_rows(u, 2)
+
+        panel = jnp.where(block_of > b, nn3(inverse, work[b] - upd[:, 0:N]), 0.0)
+        fac[...] = panel
+        fac[:, columns] = diagonal
+        here = pl.ds(pl.multiple_of(b * H, H), H)
+        fac_h[here], fac_l[here] = split(fac[...])
+        nh, nl = split(fac[:, ncolumns])
+        diag[...] = (work[later, :, ncolumns] - upd[:, N : N + H]) - tn3(nh, nl, nh, nl)
+        for q in range(4):
+            out[b, q] = fac[:, q * H : q * H + H]
 
     def lf_copy(k, b, q):
         return pltpu.make_async_remote_copy(
             src_ref=rleaf.at[b, q],
-            dst_ref=lf_out.at[k, b * H : b * H + H],
+            dst_ref=lf_out.at[k, pl.ds(b * H, H)],
             send_sem=lf_send.at[b, q],
             recv_sem=lf_recv.at[k, b],
             device_id={"row": q},
@@ -292,73 +345,47 @@
             device_id_type=MESH,
         )
 
-    work[...] = jnp.zeros_like(work)
-    fac_h[...] = jnp.zeros_like(fac_h)
-    fac_l[...] = jnp.zeros_like(fac_l)
-
     @pl.when(factors)
     def _():
+        fac_h[...] = jnp.zeros_like(fac_h)
+        fac_l[...] = jnp.zeros_like(fac_l)
+        wait_near(k_here, -1)
+        diag[...] = summed(k_here, 0) + direct[k_here]
+
         def step(b, carry):
-            @pl.when(b == 0)
-            def _():
-                for k in range(2):
-
-                    @pl.when(k_mine == k)
-                    def _(k=k):
-                        fill_rows(k, 0)
-                        fill_rows(k, 1)
-
-            @pl.when(b == 1)
-            def _():
-                for k in range(2):
-
-                    @pl.when(k_mine == k)
-                    def _(k=k):
-                        fill_rows(k, 2)
-
-            factor_rows(b, rleaf)
-            for q in range(4):
-
-                @pl.when(jnp.logical_and(q != r, q >= b))
-                def _(q=q):
-                    for k in range(2):
-                        for bb in range(2):
-
-                            @pl.when(jnp.logical_and(k_mine == k, b == bb))
-                            def _(k=k, bb=bb):
-                                lf_copy(k, bb, q).start()
-
+            factor_rows(k_here, b, rleaf)
             return carry
 
         lax.fori_loop(0, 2, step, 0)
-        for k in range(2):
-
-            @pl.when(k_mine == k)
-            def _(k=k):
-                wait_near(k, 3)
-                for b in range(2):
-
-                    for q in range(4):
-
-                        @pl.when(jnp.logical_and(q == r, q >= b))
-                        def _(q=q, b=b):
-                            lf_out[k, b * H : b * H + H] = rleaf[b, q]
-
-        for i in range(2):
-            rows = slice(256 + H * i, 384 + H * i)
-            columns = slice(256 + H * i, N)
-            left_h, left_l = fac_h[0:256, rows], fac_l[0:256, rows]
-            right_h, right_l = fac_h[0:256, columns], fac_l[0:256, columns]
-            taken = tn(left_h, right_h) + (tn(left_h, right_l) + tn(left_l, right_h))
-            for j in range(i, 2):
-                b = 7 + i + j
-                slots[2, i + j] = summed(k_mine, b) - taken[:, (j - i) * H : (j - i) * H + H]
+        slots[2, 0] = diag[...]
+        rows = slice(384, N)
+        columns = slice(256, N)
+        taken = tn3(
+            fac_h[0:256, rows], fac_l[0:256, rows], fac_h[0:256, columns], fac_l[0:256, columns]
+        )
+        slots[2, 1] = work[2, :, 384:N] - taken[:, 0:H].T
+        slots[2, 2] = work[3, :, 384:N] - taken[:, H : 2 * H]
         for delta in (-2, -1, 1, 2):
 
             @pl.when(jnp.logical_and(l + delta >= 0, l + delta < leaves))
             def _(delta=delta):
                 slot_copy(delta).start()
 
+        for q in range(4):
+            for b in range(min(q, 1) + 1):
+
+                @pl.when(q != r)
+                def _(q=q, b=b):
+                    lf_copy(k_here, b, q).start()
+
+                @pl.when(q == r)
+                def _(q=q, b=b):
+                    lf_out[k_here, b * H : b * H + H] = rleaf[b, q]
+
+    for copy in small[1:]:
+        copy.wait()
+    add_gram(ps[...], True)
+    finish_gram(2, 1.0 / (4 * ps.shape[0]))
     for k in range(2):
 
         @pl.when(r == 0)
@@ -371,9 +398,14 @@
         def _(b=b):
             pf_out[0, b * H : b * H + H] = jnp.zeros((H, H), F32)
 
+    @pl.when(place[2] == 0)
+    def _():
+        fac_h[...] = jnp.zeros_like(fac_h)
+        fac_l[...] = jnp.zeros_like(fac_l)
+
     even = lax.rem(l, 2) == r // 2
 
-    for delta in range(-REACH, REACH + 1):
+    for delta in (0, 1, -1, 2, -2):
         source = l - delta
         parity = even if delta % 2 == 0 else jnp.logical_not(even)
         valid = jnp.logical_and(parity, jnp.logical_and(source >= 0, source < leaves))
@@ -400,13 +432,13 @@
                         ii, jj = (i - 2 * half) * H, (j - 2 * half) * H
                         gram[2, b] = gram[2, b] + placed[ii : ii + H, jj : jj + H]
 
-    start_far(2)
+    start_first(2)
     forward(2)
 
     def pf_copy(b, q):
         return pltpu.make_async_remote_copy(
             src_ref=rpar.at[b, q],
-            dst_ref=pf_out.at[0, b * H : b * H + H],
+            dst_ref=pf_out.at[0, pl.ds(b * H, H)],
             send_sem=pf_send.at[b, q],
             recv_sem=pf_recv.at[b],
             device_id={"row": q},
@@ -415,32 +447,20 @@
 
     @pl.when(place[2] == 0)
     def _():
-        fac_h[...] = jnp.zeros_like(fac_h)
-        fac_l[...] = jnp.zeros_like(fac_l)
+        wait_near(2, -1)
+        diag[...] = summed(2, 0) + direct[2]
 
         def step(b, carry):
-            for ci in range(1, 4):
-
-                @pl.when(b == ci - 1)
-                def _(ci=ci):
-                    if ci == 1:
-                        fill_rows(2, 0)
-                    fill_rows(2, ci)
-            @pl.when(b == 2)
-            def _():
-                pass
-
-            factor_rows(b, rpar)
+            factor_rows(2, b, rpar)
             for q in range(4):
-                for bb in range(q + 1):
-
-                    @pl.when(jnp.logical_and(q != r, b == bb))
-                    def _(q=q, bb=bb):
-                        pf_copy(bb, q).start()
-
-                    @pl.when(jnp.logical_and(q == r, b == bb))
-                    def _(q=q, bb=bb):
-                        pf_out[0, bb * H : bb * H + H] = rpar[bb, q]
+
+                @pl.when(jnp.logical_and(q != r, q >= b))
+                def _(q=q):
+                    pf_copy(b, q).start()
+
+                @pl.when(jnp.logical_and(q == r, q >= b))
+                def _(q=q):
+                    pf_out[0, pl.ds(pl.multiple_of(b * H, H), H)] = rpar[b, q]
 
             return carry
 
@@ -449,16 +469,16 @@
 
             @pl.when(q != r)
             def _(q=q):
-                for bb in range(q + 1):
-                    pf_copy(bb, q).wait_send()
+                for b in range(q + 1):
+                    pf_copy(b, q).wait_send()
 
     @pl.when(place[2] != 0)
     def _():
-        for bb in range(4):
-
-            @pl.when(bb <= r)
-            def _(bb=bb):
-                pf_copy(bb, 0).wait_recv()
+        for b in range(4):
+
+            @pl.when(b <= r)
+            def _(b=b):
+                pf_copy(b, 0).wait_recv()
 
     for k in range(2):
 
@@ -502,15 +522,12 @@
             jax.ShapeDtypeStruct((kids, 256, H), F32),
             jax.ShapeDtypeStruct((1, N, H), F32),
         ),
-        in_specs=[
-            pl.BlockSpec(memory_space=pltpu.SMEM),
-            pl.BlockSpec(memory_space=pltpu.SMEM),
-            pl.BlockSpec(memory_space=pltpu.VMEM),
-            pl.BlockSpec(memory_space=pl.ANY),
-            pl.BlockSpec(memory_space=pl.ANY),
-        ],
+        in_specs=[pl.BlockSpec(memory_space=pl.ANY)] * 5,
         out_specs=(pl.BlockSpec(memory_space=pltpu.VMEM),) * 2,
         scratch_shapes=[
+            pltpu.SMEM(front_rows.shape, jnp.int32),
+            pltpu.SMEM(parent_of.shape, jnp.int32),
+            vmem(column_map.shape, jnp.int32),
             vmem((kids, live_rows, N), F32),
             vmem(parent_rows.shape[1:], F32),
             vmem((N, N), F32),
@@ -518,18 +535,24 @@
             vmem((3, 10, H, H), F32),
             vmem((3, 10, H // 2, H), F32),
             vmem((3, 2, 10, H, H), F32),
+            vmem((3, H, H), F32),
             vmem((4, H, N), F32),
+            vmem((H, H), F32),
+            vmem((H, N + H), F32),
             vmem((H, N), F32),
             vmem((N, N), BF16),
             vmem((N, N), BF16),
             vmem((2, 4, H, H), F32),
             vmem((4, 4, H, H), F32),
             vmem((5, 3, H, H), F32),
-            dma((3, 2)),
+            dma((2, 2)),
+            dma((4,)),
+            dma((3,)),
+            dma((3,)),
             dma((3, 2, chunks)),
             dma((3, chunks)),
-            dma((3, chunks)),
-            dma((3, 2, chunks)),
+            dma((3, chunks + 1)),
+            dma((3, 2, chunks + 1)),
             dma((2, 4)),
             dma((2, 2)),
             dma((5,)),
@@ -538,7 +561,7 @@
             dma((4,)),
         ],
         compiler_params=pltpu.CompilerParams(
-            collective_id=0, has_side_effects=True, vmem_limit_bytes=48 << 20
+            collective_id=0, has_side_effects=True, vmem_limit_bytes=60 << 20
         ),
         name="fronts",
     )(front_rows, parent_of, column_map, leaf_fronts, parent_rows)

time: 65.5 us -> 60.2 us (0.919)
  the two profiles are of different devices: /device:TPU:153 before, /device:TPU:217 now
where the time goes in v2:
time: 60.2 us; the launch traced here: 60 us
  Pallas kernels  56.1 us (93%)
  local copies, waits for them, and re-layouts  3.34 us (6%)
  between operations  0.64 us (1%)
    pallas_call x1, Pallas kernels, per_device(): pl.pallas_call(kernel, out_shape=(jax.ShapeDtypeStruct((kids, 256, H), F3...  56.1 us
    unnamed x2, local copies, waits for them, and re-layouts  3.34 us

profile of v2, /device:TPU:217, one launch (start us, length us, event | category | flops | bytes accessed | tf_op | source)
XLA Modules:
  0.0 60.0 jit_solution(3477547239714039727)
XLA Ops:
  0.6 56.1 %fronts.1 = (f32[2,256,128]{2,1,0:T(8,128)}, f32[1,512,128]{2,1,0:T(8,128)}) custom-call(s32[2]{0:T(128)} %rows_hbm.1, s32[128]{0:T(128)} %parent_hbm.1, s32[128,256]{1,0:T(8,128)} %map_hbm.1, f32[2,2048,512]{2,1,0:T(8,128)} %leaf_hbm.1, f32[1,256,512]{2,1,0:T(8,128)} %prow_hbm.1), custom_call_target="tpu_custom_call" | custom-call | tf_op jit(solution)/shard_map/fronts/pallas_call | solution.py:519
  56.7 1.7 %copy.9 = f32[2,256,128]{2,1,0:T(8,128)} copy(f32[2,256,128]{2,1,0:T(8,128)} %get-tuple-element.4) | data formatting | bytes 524288
  58.4 1.7 %copy.10 = f32[1,512,128]{2,1,0:T(8,128)} copy(f32[1,512,128]{2,1,0:T(8,128)} %get-tuple-element.5) | data formatting | bytes 524288

commit v3 on v2

--- a/solution.py
+++ b/solution.py
@@ -115,7 +115,7 @@
 def kernel(
     rows_hbm, parent_hbm, map_hbm, leaf_hbm, prow_hbm, lf_out, pf_out,
     rows_ref, parent_ref, map_ref, xs, ps, hh, hl, gram, far, near, direct,
-    work, diag, upd, fac, fac_h, fac_l, rleaf, rpar, slots,
+    work, diag, rleaf, rpar, slots,
     load_sem, small_sem, direct_send, direct_recv, far_send, far_recv, near_send, near_recv,
     lf_send, lf_recv, slot_send, slot_recv, pf_send, pf_recv,
 ):
@@ -143,13 +143,13 @@
         pl.semaphore_signal(barrier, inc=1, device_id={"row": mod4(r + step)}, device_id_type=MESH)
     greeted = 3
     for delta in (-2, -1, 1, 2):
-        inside = jnp.logical_and(l + delta >= 0, l + delta < leaves)
-
-        @pl.when(inside)
+        there = jnp.logical_and(l + delta >= 0, l + delta < leaves)
+
+        @pl.when(there)
         def _(delta=delta):
             pl.semaphore_signal(barrier, inc=1, device_id={"leaf": l + delta}, device_id_type=MESH)
 
-        greeted = greeted + jnp.where(inside, 1, 0)
+        greeted = greeted + jnp.where(there, 1, 0)
 
     def load(step, c):
         k = first if step == 0 else 1 - first
@@ -215,12 +215,13 @@
             def _(side=side):
                 near_copy(u, -1, side).start()
 
-    def forward(u):
+    def forward(u, which):
         for side in range(2):
 
             @pl.when(place[u] == 1 + 2 * side)
             def _(side=side):
-                for ci, (b0, b1) in enumerate(CHUNKS):
+                for ci in which:
+                    b0, b1 = CHUNKS[ci]
                     far_copy(u, ci, side).wait_recv()
                     half = pl.ds(64 * side, 64)
                     gram[u, b0:b1, half] = gram[u, b0:b1, half] + far[u, b0:b1]
@@ -284,46 +285,57 @@
             def _(u=u):
                 start_first(u)
 
-    forward(0)
-    forward(1)
-
-    block_of = lax.broadcasted_iota(jnp.int32, (H, N), 1) // H
-
-    def fill_rows(u, ci):
+    for u in range(2):
+        forward(u, (0, 1))
+
+    def fill_rows(u, ci, add):
         wait_near(u, ci)
         b0, b1 = CHUNKS[ci]
         for b in range(b0, b1):
             i, j = BLOCKS[b]
-            work[i, :, j * H : j * H + H] = summed(u, b)
-
-    def factor_rows(u, b, out):
-        columns = pl.ds(pl.multiple_of(b * H, H), H)
-        later = jnp.minimum(b + 1, 3)
-        ncolumns = pl.ds(pl.multiple_of(later * H, H), H)
-        whole_h, whole_l = fac_h[...], fac_l[...]
-        upd[:, 0:N] = tn3(fac_h[:, columns], fac_l[:, columns], whole_h, whole_l)
-        nh, nl = fac_h[:, ncolumns], fac_l[:, ncolumns]
-        upd[:, N : N + H] = tn3(nh, nl, nh, nl)
-        diagonal, inverse = factor_block(diag[...])
-
-        @pl.when(b == 0)
-        def _():
-            fill_rows(u, 0)
-            fill_rows(u, 1)
-
-        @pl.when(b == 1)
-        def _():
-            fill_rows(u, 2)
-
-        panel = jnp.where(block_of > b, nn3(inverse, work[b] - upd[:, 0:N]), 0.0)
-        fac[...] = panel
-        fac[:, columns] = diagonal
-        here = pl.ds(pl.multiple_of(b * H, H), H)
-        fac_h[here], fac_l[here] = split(fac[...])
-        nh, nl = split(fac[:, ncolumns])
-        diag[...] = (work[later, :, ncolumns] - upd[:, N : N + H]) - tn3(nh, nl, nh, nl)
-        for q in range(4):
-            out[b, q] = fac[:, q * H : q * H + H]
+            columns = slice(j * H, j * H + H)
+            work[i, :, columns] = work[i, :, columns] + summed(u, b) if add else summed(u, b)
+
+    def factor(u, count, out, beside, after):
+        wait_near(u, -1)
+        diag[...] = summed(u, 0) + direct[u]
+        for b in range(count):
+            diagonal, inverse = factor_block(diag[...])
+            out[b, b] = diagonal
+            beside(b)
+            if b < 3:
+                if b == 0:
+                    fill_rows(u, 0, False)
+                    fill_rows(u, 1, False)
+                if b == 1:
+                    fill_rows(u, 2, True)
+                lo = b * H + H
+                ih, il = split(inverse)
+
+                def solve(columns):
+                    wh, wl = split(work[b, :, columns])
+                    return nn(ih, wh) + (nn(ih, wl) + nn(il, wh))
+
+                near_panel = solve(slice(lo, lo + H))
+                nh, nl = split(near_panel)
+                out[b, b + 1] = near_panel
+                if b == 0:
+                    diag[...] = work[1, :, lo : lo + H] - tn3(nh, nl, nh, nl)
+                else:
+                    diag[...] = work[b + 1, :, lo : lo + H] - tn3(nh, nl, nh, nl)
+                if b < 2:
+                    rest = solve(slice(lo + H, N))
+                    rh, rl = split(rest)
+                    for q in range(b + 2, 4):
+                        out[b, q] = rest[:, (q - b - 2) * H : (q - b - 1) * H]
+                    columns = slice(lo + H, N)
+                    work[b + 1, :, columns] = work[b + 1, :, columns] - tn3(nh, nl, rh, rl)
+                    for i in range(b + 2, 4):
+                        o = (i - b - 2) * H
+                        columns = slice(i * H, N)
+                        taken = tn3(rh[:, o : o + H], rl[:, o : o + H], rh[:, o:], rl[:, o:])
+                        work[i, :, columns] = -taken if b == 0 else work[i, :, columns] - taken
+            after(b)
 
     def lf_copy(k, b, q):
         return pltpu.make_async_remote_copy(
@@ -345,32 +357,49 @@
             device_id_type=MESH,
         )
 
+    sibling = l + 1 - 2 * core
+    onward = 4 * core - 2
+
+    def slot_copy(source, slot, device, send):
+        return pltpu.make_async_remote_copy(
+            src_ref=slots.at[source],
+            dst_ref=slots.at[slot],
+            send_sem=slot_send.at[send],
+            recv_sem=slot_recv.at[slot],
+            device_id={"leaf": device},
+            device_id_type=MESH,
+        )
+
+    def inside(place_of):
+        return jnp.logical_and(place_of >= 0, place_of < leaves)
+
+    def own_slot(delta):
+        return slot_copy(2, 2 + delta, l + delta, 2 + delta)
+
+    def sibling_slot():
+        return slot_copy(2, 2 + sibling - l, sibling, 1)
+
+    def onward_slot():
+        return slot_copy(2 + onward, 1 + 2 * core, sibling, 2)
+
     @pl.when(factors)
     def _():
-        fac_h[...] = jnp.zeros_like(fac_h)
-        fac_l[...] = jnp.zeros_like(fac_l)
-        wait_near(k_here, -1)
-        diag[...] = summed(k_here, 0) + direct[k_here]
-
-        def step(b, carry):
-            factor_rows(k_here, b, rleaf)
-            return carry
-
-        lax.fori_loop(0, 2, step, 0)
+        def beside(b):
+            if b == 0:
+                for u in range(2):
+                    forward(u, (2,))
+
+        factor(k_here, 2, rleaf, beside, lambda b: None)
         slots[2, 0] = diag[...]
-        rows = slice(384, N)
-        columns = slice(256, N)
-        taken = tn3(
-            fac_h[0:256, rows], fac_l[0:256, rows], fac_h[0:256, columns], fac_l[0:256, columns]
-        )
-        slots[2, 1] = work[2, :, 384:N] - taken[:, 0:H].T
-        slots[2, 2] = work[3, :, 384:N] - taken[:, H : 2 * H]
-        for delta in (-2, -1, 1, 2):
-
-            @pl.when(jnp.logical_and(l + delta >= 0, l + delta < leaves))
+        slots[2, 1] = work[2, :, 384:N]
+        slots[2, 2] = work[3, :, 384:N]
+        for delta in (-2, 2):
+
+            @pl.when(inside(l + delta))
             def _(delta=delta):
-                slot_copy(delta).start()
-
+                own_slot(delta).start()
+
+        sibling_slot().start()
         for q in range(4):
             for b in range(min(q, 1) + 1):
 
@@ -381,6 +410,11 @@
                 @pl.when(q == r)
                 def _(q=q, b=b):
                     lf_out[k_here, b * H : b * H + H] = rleaf[b, q]
+
+    @pl.when(jnp.logical_not(factors))
+    def _():
+        for u in range(2):
+            forward(u, (2,))
 
     for copy in small[1:]:
         copy.wait()
@@ -398,27 +432,33 @@
         def _(b=b):
             pf_out[0, b * H : b * H + H] = jnp.zeros((H, H), F32)
 
-    @pl.when(place[2] == 0)
-    def _():
-        fac_h[...] = jnp.zeros_like(fac_h)
-        fac_l[...] = jnp.zeros_like(fac_l)
-
-    even = lax.rem(l, 2) == r // 2
-
-    for delta in (0, 1, -1, 2, -2):
+    def place_slot(i, carry):
+        one = 2 * core - 1
+        delta = jnp.where(
+            factors,
+            jnp.where(i == 0, 0, jnp.where(i == 1, onward, -onward)),
+            jnp.where(i == 0, one, -one),
+        )
         source = l - delta
-        parity = even if delta % 2 == 0 else jnp.logical_not(even)
-        valid = jnp.logical_and(parity, jnp.logical_and(source >= 0, source < leaves))
+        valid = jnp.logical_and(jnp.logical_or(factors, i < 2), inside(source))
 
         @pl.when(valid)
-        def _(delta=delta, source=source):
-            if delta != 0:
-                slot_copy(delta).wait_recv()
+        def _():
+            slot = 2 + delta
+
+            @pl.when(delta != 0)
+            def _():
+                slot_copy(2, slot, sibling, 0).wait_recv()
+
+            @pl.when(jnp.logical_and(factors, i == 1))
+            def _():
+                onward_slot().start()
+
             front = 2 * source + lax.rem(r, 2)
             away = jnp.where(parent_ref[front] == l, 0, 2 * N)
             target = map_ref[pl.ds(front, 1), :] + away
             chosen = (lax.broadcasted_iota(jnp.int32, (N, 256), 0) == target).astype(F32).astype(BF16)
-            s = slots[2 + delta]
+            s = slots[slot]
             square = jnp.concatenate(
                 [jnp.concatenate([s[0], s[1]], 1), jnp.concatenate([s[1].T, s[2]], 1)], 0
             )
@@ -427,13 +467,17 @@
             for half in range(2):
                 rows, columns = slice(256 * half, 256 * half + 256), slice(256 * half, N)
                 placed = nt(high_rows[rows], chosen[columns]) + nt(low_rows[rows], chosen[columns])
-                for b, (i, j) in enumerate(BLOCKS):
-                    if i // 2 == half:
-                        ii, jj = (i - 2 * half) * H, (j - 2 * half) * H
+                for b, (bi, bj) in enumerate(BLOCKS):
+                    if bi // 2 == half:
+                        ii, jj = (bi - 2 * half) * H, (bj - 2 * half) * H
                         gram[2, b] = gram[2, b] + placed[ii : ii + H, jj : jj + H]
 
+        return carry
+
+    lax.fori_loop(0, 3, place_slot, 0)
+
     start_first(2)
-    forward(2)
+    forward(2, (0, 1, 2))
 
     def pf_copy(b, q):
         return pltpu.make_async_remote_copy(
@@ -447,24 +491,18 @@
 
     @pl.when(place[2] == 0)
     def _():
-        wait_near(2, -1)
-        diag[...] = summed(2, 0) + direct[2]
-
-        def step(b, carry):
-            factor_rows(2, b, rpar)
-            for q in range(4):
-
-                @pl.when(jnp.logical_and(q != r, q >= b))
+        def after(b):
+            for q in range(b, 4):
+
+                @pl.when(q != r)
                 def _(q=q):
                     pf_copy(b, q).start()
 
-                @pl.when(jnp.logical_and(q == r, q >= b))
+                @pl.when(q == r)
                 def _(q=q):
-                    pf_out[0, pl.ds(pl.multiple_of(b * H, H), H)] = rpar[b, q]
-
-            return carry
-
-        lax.fori_loop(0, 4, step, 0)
+                    pf_out[0, b * H : b * H + H] = rpar[b, q]
+
+        factor(2, 4, rpar, lambda b: None, after)
         for q in range(4):
 
             @pl.when(q != r)
@@ -501,11 +539,17 @@
 
     @pl.when(factors)
     def _():
-        for delta in (-2, -1, 1, 2):
-
-            @pl.when(jnp.logical_and(l + delta >= 0, l + delta < leaves))
+        for delta in (-2, 2):
+
+            @pl.when(inside(l + delta))
             def _(delta=delta):
-                slot_copy(delta).wait_send()
+                own_slot(delta).wait_send()
+
+        sibling_slot().wait_send()
+
+        @pl.when(inside(l - onward))
+        def _():
+            onward_slot().wait_send()
 
     for u in range(3):
         drain(u)
@@ -522,7 +566,7 @@
             jax.ShapeDtypeStruct((kids, 256, H), F32),
             jax.ShapeDtypeStruct((1, N, H), F32),
         ),
-        in_specs=[pl.BlockSpec(memory_space=pl.ANY)] * 5,
+        in_specs=[pl.BlockSpec(memory_space=pltpu.HBM)] * 5,
         out_specs=(pl.BlockSpec(memory_space=pltpu.VMEM),) * 2,
         scratch_shapes=[
             pltpu.SMEM(front_rows.shape, jnp.int32),
@@ -538,10 +582,6 @@
             vmem((3, H, H), F32),
             vmem((4, H, N), F32),
             vmem((H, H), F32),
-            vmem((H, N + H), F32),
-            vmem((H, N), F32),
-            vmem((N, N), BF16),
-            vmem((N, N), BF16),
             vmem((2, 4, H, H), F32),
             vmem((4, 4, H, H), F32),
             vmem((5, 3, H, H), F32),

time: 60.2 us -> 57.9 us (0.962)
  the two profiles are of different devices: /device:TPU:217 before, /device:TPU:176 now
where the time goes in v3:
time: 57.9 us; the launch traced here: 57.1 us
  Pallas kernels  53.2 us (92%)
  local copies, waits for them, and re-layouts  3.34 us (6%)
  between operations  0.64 us (1%)
    pallas_call x1, Pallas kernels, per_device(): pl.pallas_call(kernel, out_shape=(jax.ShapeDtypeStruct((kids, 256, H), F3...  53.2 us
    unnamed x2, local copies, waits for them, and re-layouts  3.34 us

profile of v3, /device:TPU:176, one launch (start us, length us, event | category | flops | bytes accessed | tf_op | source)
XLA Modules:
  0.0 57.1 jit_solution(16241240115763335011)
XLA Ops:
  0.6 53.2 %fronts.1 = (f32[2,256,128]{2,1,0:T(8,128)}, f32[1,512,128]{2,1,0:T(8,128)}) custom-call(s32[2]{0:T(128)} %rows_hbm.1, s32[128]{0:T(128)} %parent_hbm.1, s32[128,256]{1,0:T(8,128)} %map_hbm.1, f32[2,2048,512]{2,1,0:T(8,128)} %leaf_hbm.1, f32[1,256,512]{2,1,0:T(8,128)} %prow_hbm.1), custom_call_target="tpu_custom_call" | custom-call | tf_op jit(solution)/shard_map/fronts/pallas_call | solution.py:563
  53.8 1.7 %copy.9 = f32[2,256,128]{2,1,0:T(8,128)} copy(f32[2,256,128]{2,1,0:T(8,128)} %get-tuple-element.4) | data formatting | bytes 524288
  55.5 1.7 %copy.10 = f32[1,512,128]{2,1,0:T(8,128)} copy(f32[1,512,128]{2,1,0:T(8,128)} %get-tuple-element.5) | data formatting | bytes 524288

commit v4 on v3

--- a/solution.py
+++ b/solution.py
@@ -205,9 +205,8 @@
         @pl.when(place[u] == 2)
         def _():
             direct_copy(u).start()
-            for ci in range(len(CHUNKS)):
-                for side in range(2):
-                    far_copy(u, ci, side).start()
+            for side in range(2):
+                far_copy(u, 0, side).start()
 
         for side in range(2):
 
@@ -215,7 +214,14 @@
             def _(side=side):
                 near_copy(u, -1, side).start()
 
-    def forward(u, which):
+    def next_far(u, ci):
+        @pl.when(place[u] == 2)
+        def _():
+            for side in range(2):
+                far_copy(u, ci - 1, side).wait_send()
+                far_copy(u, ci, side).start()
+
+    def forward(u, which, waits):
         for side in range(2):
 
             @pl.when(place[u] == 1 + 2 * side)
@@ -225,6 +231,19 @@
                     far_copy(u, ci, side).wait_recv()
                     half = pl.ds(64 * side, 64)
                     gram[u, b0:b1, half] = gram[u, b0:b1, half] + far[u, b0:b1]
+                    if ci == 1:
+
+                        @pl.when(waits)
+                        def _():
+                            near_copy(u, 0, side).wait_send()
+
+                    if ci == 2:
+
+                        @pl.when(jnp.logical_not(waits))
+                        def _():
+                            near_copy(u, 0, side).wait_send()
+
+                        near_copy(u, 1, side).wait_send()
                     near_copy(u, ci, side).start()
 
     def wait_near(u, ci):
@@ -237,15 +256,14 @@
         @pl.when(place[u] == 2)
         def _():
             direct_copy(u).wait_send()
-            for ci in range(len(CHUNKS)):
-                for side in range(2):
-                    far_copy(u, ci, side).wait_send()
+            for side in range(2):
+                far_copy(u, 2, side).wait_send()
 
         for side in range(2):
 
             @pl.when(place[u] == 1 + 2 * side)
             def _(side=side):
-                for ci in range(-1, len(CHUNKS)):
+                for ci in (-1, 2):
                     near_copy(u, ci, side).wait_send()
 
     def summed(u, b):
@@ -276,6 +294,9 @@
             x = xs[k, pl.ds(c * piece, piece)]
             position = lax.broadcasted_iota(jnp.int32, (piece, N), 0) + c * piece
             add_gram(jnp.where(position < live, x, 0.0), c == 0)
+            if step == 1 and c < 2:
+                for u in range(2):
+                    next_far(u, c + 1)
         finish_gram(k, 1.0 / total)
         if step == 0:
             pl.semaphore_wait(barrier, greeted)
@@ -286,7 +307,7 @@
                 start_first(u)
 
     for u in range(2):
-        forward(u, (0, 1))
+        forward(u, (0, 1), jnp.logical_not(factors))
 
     def fill_rows(u, ci, add):
         wait_near(u, ci)
@@ -387,7 +408,7 @@
         def beside(b):
             if b == 0:
                 for u in range(2):
-                    forward(u, (2,))
+                    forward(u, (2,), jnp.logical_not(factors))
 
         factor(k_here, 2, rleaf, beside, lambda b: None)
         slots[2, 0] = diag[...]
@@ -400,21 +421,10 @@
                 own_slot(delta).start()
 
         sibling_slot().start()
-        for q in range(4):
-            for b in range(min(q, 1) + 1):
-
-                @pl.when(q != r)
-                def _(q=q, b=b):
-                    lf_copy(k_here, b, q).start()
-
-                @pl.when(q == r)
-                def _(q=q, b=b):
-                    lf_out[k_here, b * H : b * H + H] = rleaf[b, q]
-
     @pl.when(jnp.logical_not(factors))
     def _():
         for u in range(2):
-            forward(u, (2,))
+            forward(u, (2,), jnp.logical_not(factors))
 
     for copy in small[1:]:
         copy.wait()
@@ -431,6 +441,19 @@
         @pl.when(b > r)
         def _(b=b):
             pf_out[0, b * H : b * H + H] = jnp.zeros((H, H), F32)
+
+    @pl.when(factors)
+    def _():
+        for q in range(4):
+            for b in range(min(q, 1) + 1):
+
+                @pl.when(q != r)
+                def _(q=q, b=b):
+                    lf_copy(k_here, b, q).start()
+
+                @pl.when(q == r)
+                def _(q=q, b=b):
+                    lf_out[k_here, b * H : b * H + H] = rleaf[b, q]
 
     def place_slot(i, carry):
         one = 2 * core - 1
@@ -477,7 +500,9 @@
     lax.fori_loop(0, 3, place_slot, 0)
 
     start_first(2)
-    forward(2, (0, 1, 2))
+    for ci in (1, 2):
+        next_far(2, ci)
+    forward(2, (0, 1, 2), l >= 0)
 
     def pf_copy(b, q):
         return pltpu.make_async_remote_copy(

time: 57.9 us -> 61.8 us (1.067)
  Pallas kernels: 53.2 us -> 56.7 us
    pallas_call x1, Pallas kernels: 53.2 us -> 56.7 us  [per_device(): pl.pallas_call(kernel, out_shape=(jax.ShapeDtypeStruct((kids, 256, H), F3...]
where the time goes in v4:
time: 61.8 us; the launch traced here: 60.7 us
  Pallas kernels  56.7 us (92%)
  local copies, waits for them, and re-layouts  3.34 us (5%)
  between operations  0.64 us (1%)
    pallas_call x1, Pallas kernels, per_device(): pl.pallas_call(kernel, out_shape=(jax.ShapeDtypeStruct((kids, 256, H), F3...  56.7 us
    unnamed x2, local copies, waits for them, and re-layouts  3.34 us

profile of v4, /device:TPU:176, one launch (start us, length us, event | category | flops | bytes accessed | tf_op | source)
XLA Modules:
  0.0 60.7 jit_solution(12075269605187943495)
XLA Ops:
  0.6 56.7 %fronts.1 = (f32[2,256,128]{2,1,0:T(8,128)}, f32[1,512,128]{2,1,0:T(8,128)}) custom-call(s32[2]{0:T(128)} %rows_hbm.1, s32[128]{0:T(128)} %parent_hbm.1, s32[128,256]{1,0:T(8,128)} %map_hbm.1, f32[2,2048,512]{2,1,0:T(8,128)} %leaf_hbm.1, f32[1,256,512]{2,1,0:T(8,128)} %prow_hbm.1), custom_call_target="tpu_custom_call" | custom-call | tf_op jit(solution)/shard_map/fronts/pallas_call | solution.py:588
  57.3 1.7 %copy.9 = f32[2,256,128]{2,1,0:T(8,128)} copy(f32[2,256,128]{2,1,0:T(8,128)} %get-tuple-element.4) | data formatting | bytes 524288
  59.0 1.7 %copy.10 = f32[1,512,128]{2,1,0:T(8,128)} copy(f32[1,512,128]{2,1,0:T(8,128)} %get-tuple-element.5) | data formatting | bytes 524288

commit v5 on v4

--- a/solution.py
+++ b/solution.py
@@ -10,7 +10,7 @@
 N = 512
 H = 128
 BLOCKS = [(i, j) for i in range(4) for j in range(i, 4)]
-CHUNKS = ((1, 4), (4, 7), (7, 10))
+CHUNKS = ((1, 5), (5, 7), (7, 10))
 REACH = 2
 
 
@@ -132,7 +132,7 @@
 
     place = [mod4(r - (2 * core + k)) for k in range(2)]
     first = jnp.where(jnp.logical_or(place[0] == 0, place[0] == 3), 1, 0)
-    rp = 3 - 2 * core
+    rp = core
     place.append(mod4(r - rp))
     k_mine = r - 2 * core
     factors = jnp.logical_and(k_mine >= 0, k_mine < 2)
@@ -218,7 +218,6 @@
         @pl.when(place[u] == 2)
         def _():
             for side in range(2):
-                far_copy(u, ci - 1, side).wait_send()
                 far_copy(u, ci, side).start()
 
     def forward(u, which, waits):
@@ -231,19 +230,8 @@
                     far_copy(u, ci, side).wait_recv()
                     half = pl.ds(64 * side, 64)
                     gram[u, b0:b1, half] = gram[u, b0:b1, half] + far[u, b0:b1]
-                    if ci == 1:
-
-                        @pl.when(waits)
-                        def _():
-                            near_copy(u, 0, side).wait_send()
-
-                    if ci == 2:
-
-                        @pl.when(jnp.logical_not(waits))
-                        def _():
-                            near_copy(u, 0, side).wait_send()
-
-                        near_copy(u, 1, side).wait_send()
+                    if waits and ci:
+                        near_copy(u, ci - 2, side).wait_send()
                     near_copy(u, ci, side).start()
 
     def wait_near(u, ci):
@@ -256,14 +244,15 @@
         @pl.when(place[u] == 2)
         def _():
             direct_copy(u).wait_send()
-            for side in range(2):
-                far_copy(u, 2, side).wait_send()
+            for ci in range(len(CHUNKS)):
+                for side in range(2):
+                    far_copy(u, ci, side).wait_send()
 
         for side in range(2):
 
             @pl.when(place[u] == 1 + 2 * side)
             def _(side=side):
-                for ci in (-1, 2):
+                for ci in (1, 2) if u == 2 else range(-1, 3):
                     near_copy(u, ci, side).wait_send()
 
     def summed(u, b):
@@ -307,10 +296,11 @@
                 start_first(u)
 
     for u in range(2):
-        forward(u, (0, 1), jnp.logical_not(factors))
-
-    def fill_rows(u, ci, add):
+        forward(u, (0, 1), False)
+
+    def fill_rows(u, ci):
         wait_near(u, ci)
+        add = ci > 0
         b0, b1 = CHUNKS[ci]
         for b in range(b0, b1):
             i, j = BLOCKS[b]
@@ -326,10 +316,10 @@
             beside(b)
             if b < 3:
                 if b == 0:
-                    fill_rows(u, 0, False)
-                    fill_rows(u, 1, False)
+                    fill_rows(u, 0)
                 if b == 1:
-                    fill_rows(u, 2, True)
+                    fill_rows(u, 1)
+                    fill_rows(u, 2)
                 lo = b * H + H
                 ih, il = split(inverse)
 
@@ -340,17 +330,15 @@
                 near_panel = solve(slice(lo, lo + H))
                 nh, nl = split(near_panel)
                 out[b, b + 1] = near_panel
-                if b == 0:
-                    diag[...] = work[1, :, lo : lo + H] - tn3(nh, nl, nh, nl)
-                else:
-                    diag[...] = work[b + 1, :, lo : lo + H] - tn3(nh, nl, nh, nl)
+                diag[...] = work[b + 1, :, lo : lo + H] - tn3(nh, nl, nh, nl)
                 if b < 2:
                     rest = solve(slice(lo + H, N))
                     rh, rl = split(rest)
                     for q in range(b + 2, 4):
                         out[b, q] = rest[:, (q - b - 2) * H : (q - b - 1) * H]
                     columns = slice(lo + H, N)
-                    work[b + 1, :, columns] = work[b + 1, :, columns] - tn3(nh, nl, rh, rl)
+                    taken = tn3(nh, nl, rh, rl)
+                    work[b + 1, :, columns] = -taken if b == 0 else work[b + 1, :, columns] - taken
                     for i in range(b + 2, 4):
                         o = (i - b - 2) * H
                         columns = slice(i * H, N)
@@ -408,7 +396,7 @@
         def beside(b):
             if b == 0:
                 for u in range(2):
-                    forward(u, (2,), jnp.logical_not(factors))
+                    forward(u, (2,), False)
 
         factor(k_here, 2, rleaf, beside, lambda b: None)
         slots[2, 0] = diag[...]
@@ -424,7 +412,7 @@
     @pl.when(jnp.logical_not(factors))
     def _():
         for u in range(2):
-            forward(u, (2,), jnp.logical_not(factors))
+            forward(u, (2,), False)
 
     for copy in small[1:]:
         copy.wait()
@@ -502,7 +490,7 @@
     start_first(2)
     for ci in (1, 2):
         next_far(2, ci)
-    forward(2, (0, 1, 2), l >= 0)
+    forward(2, (0, 1, 2), True)
 
     def pf_copy(b, q):
         return pltpu.make_async_remote_copy(
@@ -580,12 +568,27 @@
         drain(u)
 
 
+def hand_over(leaf_in, parent_in, leaf_out, parent_out, sems):
+    copies = [
+        pltpu.make_async_copy(source.at[part], target.at[part], sems.at[i, j])
+        for i, (source, target, parts) in enumerate((
+            (leaf_in, leaf_out, [(k, pl.ds(h * H, H)) for k in range(2) for h in range(2)]),
+            (parent_in, parent_out, [(0, pl.ds(h * H, H)) for h in range(4)]),
+        ))
+        for j, part in enumerate(parts)
+    ]
+    for copy in copies:
+        copy.start()
+    for copy in copies:
+        copy.wait()
+
+
 def per_device(leaf_fronts, front_rows, parent_of, column_map, parent_rows):
     kids, live_rows, _ = leaf_fronts.shape
     chunks = len(CHUNKS)
     dma = pltpu.SemaphoreType.DMA
     vmem = pltpu.VMEM
-    return pl.pallas_call(
+    factors = pl.pallas_call(
         kernel,
         out_shape=(
             jax.ShapeDtypeStruct((kids, 256, H), F32),
@@ -630,6 +633,15 @@
         ),
         name="fronts",
     )(front_rows, parent_of, column_map, leaf_fronts, parent_rows)
+    hbm = pl.BlockSpec(memory_space=pltpu.HBM)
+    return pl.pallas_call(
+        hand_over,
+        out_shape=[jax.ShapeDtypeStruct(x.shape, x.dtype) for x in factors],
+        in_specs=[hbm] * 2,
+        out_specs=[hbm] * 2,
+        scratch_shapes=[dma((2, 4))],
+        name="hand_over",
+    )(*factors)
 
 
 def solution(mesh):

time: 61.8 us -> 70.5 us (1.14)
  the two profiles are of different devices: /device:TPU:176 before, /device:TPU:216 now
where the time goes in v5:
time: 70.5 us; the launch traced here: 70.4 us
  Pallas kernels  69.6 us (99%)
  between operations  0.82 us (1%)
    pallas_call x1, Pallas kernels, per_device(): pl.pallas_call(kernel, out_shape=(jax.ShapeDtypeStruct((kids, 256, H), F3...  52.5 us
    pallas_call x1, Pallas kernels, per_device(): pl.pallas_call(hand_over, out_shape=[jax.ShapeDtypeStruct(x.shape, x.dtyp...  17.1 us

profile of v5, /device:TPU:216, one launch (start us, length us, event | category | flops | bytes accessed | tf_op | source)
XLA Modules:
  0.0 70.4 jit_solution(5543195749465323915)
XLA Ops:
  0.6 52.5 %fronts.1 = (f32[2,256,128]{2,1,0:T(8,128)}, f32[1,512,128]{2,1,0:T(8,128)}) custom-call(s32[2]{0:T(128)} %rows_hbm.1, s32[128]{0:T(128)} %parent_hbm.1, s32[128,256]{1,0:T(8,128)} %map_hbm.1, f32[2,2048,512]{2,1,0:T(8,128)} %leaf_hbm.1, f32[1,256,512]{2,1,0:T(8,128)} %prow_hbm.1), custom_call_target="tpu_custom_call" | custom-call | tf_op jit(solution)/shard_map/fronts/pallas_call | solution.py:591
  53.2 17.1 %hand_over.1 = (f32[2,256,128]{2,1,0:T(8,128)}, f32[1,512,128]{2,1,0:T(8,128)}) custom-call(f32[2,256,128]{2,1,0:T(8,128)} %get-tuple-element.4.leaf_in, f32[1,512,128]{2,1,0:T(8,128)} %get-tuple-element.5.parent_in), custom_call_target="tpu_custom_call" | custom-call | tf_op jit(solution)/shard_map/hand_over/pallas_call | solution.py:637

commit v6 on v5

--- a/solution.py
+++ b/solution.py
@@ -130,11 +130,12 @@
     def mod4(v):
         return lax.rem(v + 8, 4)
 
-    place = [mod4(r - (2 * core + k)) for k in range(2)]
+    base = 2 - 2 * core
+    place = [mod4(r - (base + k)) for k in range(2)]
     first = jnp.where(jnp.logical_or(place[0] == 0, place[0] == 3), 1, 0)
-    rp = core
+    rp = 3 - core
     place.append(mod4(r - rp))
-    k_mine = r - 2 * core
+    k_mine = r - base
     factors = jnp.logical_and(k_mine >= 0, k_mine < 2)
     k_here = jnp.clip(k_mine, 0, 1)
 
@@ -568,18 +569,24 @@
         drain(u)
 
 
-def hand_over(leaf_in, parent_in, leaf_out, parent_out, sems):
-    copies = [
-        pltpu.make_async_copy(source.at[part], target.at[part], sems.at[i, j])
-        for i, (source, target, parts) in enumerate((
-            (leaf_in, leaf_out, [(k, pl.ds(h * H, H)) for k in range(2) for h in range(2)]),
-            (parent_in, parent_out, [(0, pl.ds(h * H, H)) for h in range(4)]),
-        ))
-        for j, part in enumerate(parts)
+def hand_over(leaf_in, parent_in, leaf_out, parent_out, leaf_held, parent_held, sems):
+    parts = [
+        (leaf_in, leaf_held, leaf_out, (k, pl.ds(h * H, H))) for k in range(2) for h in range(2)
+    ] + [(parent_in, parent_held, parent_out, (0, pl.ds(h * H, H))) for h in range(4)]
+    inward = [
+        pltpu.make_async_copy(source.at[part], held.at[part], sems.at[0, i])
+        for i, (source, held, target, part) in enumerate(parts)
     ]
-    for copy in copies:
+    outward = [
+        pltpu.make_async_copy(held.at[part], target.at[part], sems.at[1, i])
+        for i, (source, held, target, part) in enumerate(parts)
+    ]
+    for copy in inward:
         copy.start()
-    for copy in copies:
+    for arrived, copy in zip(inward, outward):
+        arrived.wait()
+        copy.start()
+    for copy in outward:
         copy.wait()
 
 
@@ -639,7 +646,7 @@
         out_shape=[jax.ShapeDtypeStruct(x.shape, x.dtype) for x in factors],
         in_specs=[hbm] * 2,
         out_specs=[hbm] * 2,
-        scratch_shapes=[dma((2, 4))],
+        scratch_shapes=[vmem(x.shape, x.dtype) for x in factors] + [dma((2, 8))],
         name="hand_over",
     )(*factors)
 

time: 70.5 us -> 53 us (0.75)
  the two profiles are of different devices: /device:TPU:216 before, /device:TPU:176 now
where the time goes in v6:
time: 53 us; the launch traced here: 52.8 us
  Pallas kernels  52 us (98%)
  between operations  0.82 us (2%)
    pallas_call x1, Pallas kernels, per_device(): pl.pallas_call(kernel, out_shape=(jax.ShapeDtypeStruct((kids, 256, H), F3...  50.2 us
    pallas_call x1, Pallas kernels, per_device(): pl.pallas_call(hand_over, out_shape=[jax.ShapeDtypeStruct(x.shape, x.dtyp...  1.83 us

profile of v6, /device:TPU:176, one launch (start us, length us, event | category | flops | bytes accessed | tf_op | source)
XLA Modules:
  0.0 52.8 jit_solution(3308697335784850494)
XLA Ops:
  0.6 50.2 %fronts.1 = (f32[2,256,128]{2,1,0:T(8,128)}, f32[1,512,128]{2,1,0:T(8,128)}) custom-call(s32[2]{0:T(128)} %rows_hbm.1, s32[128]{0:T(128)} %parent_hbm.1, s32[128,256]{1,0:T(8,128)} %map_hbm.1, f32[2,2048,512]{2,1,0:T(8,128)} %leaf_hbm.1, f32[1,256,512]{2,1,0:T(8,128)} %prow_hbm.1), custom_call_target="tpu_custom_call" | custom-call | tf_op jit(solution)/shard_map/fronts/pallas_call | solution.py:598
  50.8 1.8 %hand_over.1 = (f32[2,256,128]{2,1,0:T(8,128)}, f32[1,512,128]{2,1,0:T(8,128)}) custom-call(f32[2,256,128]{2,1,0:T(8,128)} %get-tuple-element.4.leaf_in, f32[1,512,128]{2,1,0:T(8,128)} %get-tuple-element.5.parent_in), custom_call_target="tpu_custom_call" | custom-call | tf_op jit(solution)/shard_map/hand_over/pallas_call | solution.py:644

commit v7 on v6

--- a/solution.py
+++ b/solution.py
@@ -61,55 +61,53 @@
     return terms[0]
 
 
-def factor_block(a):
+def factor_block(a, wanted=2):
     sub = lax.broadcasted_iota(jnp.int32, (8, H), 0)
     lane = lax.broadcasted_iota(jnp.int32, (8, H), 1)
     count = H // 8
-    tiles = [[a[8 * t : 8 * t + 8, :], (lane == sub + 8 * t).astype(F32)] for t in range(count)]
-    factor, inverse = [], []
+    tiles = [
+        [a[8 * t : 8 * t + 8, :], (lane == sub + 8 * t).astype(F32)][:wanted] for t in range(count)
+    ]
+    results = []
     for t in range(count):
         j = 8 * t
-        left, right = tiles[t]
-        column = [spread_column(left, j + k) for k in range(8)]
+        now = tiles[t]
+        column = [spread_column(now[0], j + k) for k in range(8)]
         if t + 1 < count:
             following = [spread_column(tiles[t + 1][0], j + k) for k in range(8)]
-        frow = jnp.zeros((8, H), F32)
-        irow = jnp.zeros((8, H), F32)
+        rows = [jnp.zeros((8, H), F32) for _ in now]
         for p in range(8):
             here = sub == p
             pivot = spread_row(column[p], p)
             inv = 1.0 / pivot
             root = lax.rsqrt(pivot)
-
             signed = jnp.where(here, -1.0, column[p])
 
             def eliminate(z):
                 return jnp.where(here, 0.0, z) - (signed * spread_row(z, p)) * inv
 
-            frow = jnp.where(here, left * root, frow)
-            irow = jnp.where(here, right * root, irow)
+            rows = [jnp.where(here, x * root, kept) for x, kept in zip(now, rows)]
             for k in range(p + 1, 8):
                 column[k] = eliminate(column[k])
-            left, right = eliminate(left), eliminate(right)
-        factor.append(jnp.where(lane >= sub + j, frow, 0.0))
-        inverse.append(irow)
+            now = [eliminate(x) for x in now]
+        results.append([jnp.where(lane >= sub + j, rows[0], 0.0)] + rows[1:])
         if t + 1 < count:
             nxt = [
                 old - tree([following[p] * spread_row(new, p) for p in range(8)])
-                for old, new in zip(tiles[t + 1], (left, right))
+                for old, new in zip(tiles[t + 1], now)
             ]
             if t + 2 < count:
                 below = jnp.concatenate([tiles[u][0] for u in range(t + 2, count)], 0)
-                parts = [jnp.concatenate([left, right], 1)]
+                parts = [jnp.concatenate(now, 1)] if wanted > 1 else list(now)
                 if j:
-                    parts = [jnp.zeros((j, 2 * H), F32)] + parts
-                parts.append(jnp.zeros((H - 8 - j, 2 * H), F32))
+                    parts = [jnp.zeros((j, wanted * H), F32)] + parts
+                parts.append(jnp.zeros((H - 8 - j, wanted * H), F32))
                 change = nn3_stacked(below, jnp.concatenate(parts, 0))
                 for u in range(t + 2, count):
-                    rows = change[8 * (u - t - 2) : 8 * (u - t - 1)]
-                    tiles[u] = [tiles[u][0] - rows[:, :H], tiles[u][1] - rows[:, H:]]
+                    taken = change[8 * (u - t - 2) : 8 * (u - t - 1)]
+                    tiles[u] = [x - taken[:, i * H : i * H + H] for i, x in enumerate(tiles[u])]
             tiles[t + 1] = nxt
-    return jnp.concatenate(factor, 0), jnp.concatenate(inverse, 0)
+    return [jnp.concatenate(x, 0) for x in zip(*results)]
 
 
 def kernel(
@@ -206,8 +204,6 @@
         @pl.when(place[u] == 2)
         def _():
             direct_copy(u).start()
-            for side in range(2):
-                far_copy(u, 0, side).start()
 
         for side in range(2):
 
@@ -269,8 +265,9 @@
             value = tn(high[:, rows], other[:, columns])
             ref[rows, columns] = value if start else ref[rows, columns] + value
 
-    def finish_gram(u, scale):
-        for b, (i, j) in enumerate(BLOCKS):
+    def finish_gram(u, scale, b0, b1):
+        for b in range(b0, b1):
+            i, j = BLOCKS[b]
             rows, columns = slice(H * i, H * i + H), slice(H * j, H * j + H)
             gram[u, b] = (hh[rows, columns] + (hl[rows, columns] + hl[columns, rows].T)) * scale
 
@@ -287,7 +284,7 @@
             if step == 1 and c < 2:
                 for u in range(2):
                     next_far(u, c + 1)
-        finish_gram(k, 1.0 / total)
+        finish_gram(k, 1.0 / total, 0, 1)
         if step == 0:
             pl.semaphore_wait(barrier, greeted)
         for u in range(2):
@@ -296,8 +293,13 @@
             def _(u=u):
                 start_first(u)
 
+        finish_gram(k, 1.0 / total, 1, 10)
+        if step == 0:
+            for u in range(2):
+                next_far(u, 0)
+
     for u in range(2):
-        forward(u, (0, 1), False)
+        forward(u, (0,), False)
 
     def fill_rows(u, ci):
         wait_near(u, ci)
@@ -312,7 +314,7 @@
         wait_near(u, -1)
         diag[...] = summed(u, 0) + direct[u]
         for b in range(count):
-            diagonal, inverse = factor_block(diag[...])
+            diagonal, *inverse = factor_block(diag[...], 1 if b == 3 else 2)
             out[b, b] = diagonal
             beside(b)
             if b < 3:
@@ -322,7 +324,7 @@
                     fill_rows(u, 1)
                     fill_rows(u, 2)
                 lo = b * H + H
-                ih, il = split(inverse)
+                ih, il = split(inverse[0])
 
                 def solve(columns):
                     wh, wl = split(work[b, :, columns])
@@ -397,7 +399,7 @@
         def beside(b):
             if b == 0:
                 for u in range(2):
-                    forward(u, (2,), False)
+                    forward(u, (1, 2), False)
 
         factor(k_here, 2, rleaf, beside, lambda b: None)
         slots[2, 0] = diag[...]
@@ -413,12 +415,12 @@
     @pl.when(jnp.logical_not(factors))
     def _():
         for u in range(2):
-            forward(u, (2,), False)
+            forward(u, (1, 2), False)
 
     for copy in small[1:]:
         copy.wait()
     add_gram(ps[...], True)
-    finish_gram(2, 1.0 / (4 * ps.shape[0]))
+    finish_gram(2, 1.0 / (4 * ps.shape[0]), 0, 10)
     for k in range(2):
 
         @pl.when(r == 0)
@@ -489,7 +491,7 @@
     lax.fori_loop(0, 3, place_slot, 0)
 
     start_first(2)
-    for ci in (1, 2):
+    for ci in (0, 1, 2):
         next_far(2, ci)
     forward(2, (0, 1, 2), True)
 

time: 53 us -> 54.4 us (1.026)
  Pallas kernels: 52 us -> 53.4 us
    pallas_call x1, Pallas kernels: 50.2 us -> 51.6 us  [per_device(): pl.pallas_call(kernel, out_shape=(jax.ShapeDtypeStruct((kids, 256, H), F3...]
where the time goes in v7:
time: 54.4 us; the launch traced here: 54.2 us
  Pallas kernels  53.4 us (98%)
  between operations  0.82 us (2%)
    pallas_call x1, Pallas kernels, per_device(): pl.pallas_call(kernel, out_shape=(jax.ShapeDtypeStruct((kids, 256, H), F3...  51.6 us
    pallas_call x1, Pallas kernels, per_device(): pl.pallas_call(hand_over, out_shape=[jax.ShapeDtypeStruct(x.shape, x.dtyp...  1.83 us

profile of v7, /device:TPU:176, one launch (start us, length us, event | category | flops | bytes accessed | tf_op | source)
XLA Modules:
  0.0 54.2 jit_solution(8925885370336625088)
XLA Ops:
  0.6 51.6 %fronts.1 = (f32[2,256,128]{2,1,0:T(8,128)}, f32[1,512,128]{2,1,0:T(8,128)}) custom-call(s32[2]{0:T(128)} %rows_hbm.1, s32[128]{0:T(128)} %parent_hbm.1, s32[128,256]{1,0:T(8,128)} %map_hbm.1, f32[2,2048,512]{2,1,0:T(8,128)} %leaf_hbm.1, f32[1,256,512]{2,1,0:T(8,128)} %prow_hbm.1), custom_call_target="tpu_custom_call" | custom-call | tf_op jit(solution)/shard_map/fronts/pallas_call | solution.py:600
  52.2 1.8 %hand_over.1 = (f32[2,256,128]{2,1,0:T(8,128)}, f32[1,512,128]{2,1,0:T(8,128)}) custom-call(f32[2,256,128]{2,1,0:T(8,128)} %get-tuple-element.4.leaf_in, f32[1,512,128]{2,1,0:T(8,128)} %get-tuple-element.5.parent_in), custom_call_target="tpu_custom_call" | custom-call | tf_op jit(solution)/shard_map/hand_over/pallas_call | solution.py:646

commit v8 on v7

--- a/solution.py
+++ b/solution.py
@@ -299,7 +299,7 @@
                 next_far(u, 0)
 
     for u in range(2):
-        forward(u, (0,), False)
+        forward(u, (0, 1), False)
 
     def fill_rows(u, ci):
         wait_near(u, ci)
@@ -399,7 +399,7 @@
         def beside(b):
             if b == 0:
                 for u in range(2):
-                    forward(u, (1, 2), False)
+                    forward(u, (2,), False)
 
         factor(k_here, 2, rleaf, beside, lambda b: None)
         slots[2, 0] = diag[...]
@@ -415,7 +415,7 @@
     @pl.when(jnp.logical_not(factors))
     def _():
         for u in range(2):
-            forward(u, (1, 2), False)
+            forward(u, (2,), False)
 
     for copy in small[1:]:
         copy.wait()

time: 54.4 us -> 53.1 us (0.976)
  Pallas kernels: 53.4 us -> 52.1 us
    pallas_call x1, Pallas kernels: 51.6 us -> 50.3 us  [per_device(): pl.pallas_call(kernel, out_shape=(jax.ShapeDtypeStruct((kids, 256, H), F3...]
where the time goes in v8:
time: 53.1 us; the launch traced here: 52.9 us
  Pallas kernels  52.1 us (98%)
  between operations  0.82 us (2%)
    pallas_call x1, Pallas kernels, per_device(): pl.pallas_call(kernel, out_shape=(jax.ShapeDtypeStruct((kids, 256, H), F3...  50.3 us
    pallas_call x1, Pallas kernels, per_device(): pl.pallas_call(hand_over, out_shape=[jax.ShapeDtypeStruct(x.shape, x.dtyp...  1.83 us

profile of v8, /device:TPU:176, one launch (start us, length us, event | category | flops | bytes accessed | tf_op | source)
XLA Modules:
  0.0 52.9 jit_solution(15340707866953531842)
XLA Ops:
  0.6 50.3 %fronts.1 = (f32[2,256,128]{2,1,0:T(8,128)}, f32[1,512,128]{2,1,0:T(8,128)}) custom-call(s32[2]{0:T(128)} %rows_hbm.1, s32[128]{0:T(128)} %parent_hbm.1, s32[128,256]{1,0:T(8,128)} %map_hbm.1, f32[2,2048,512]{2,1,0:T(8,128)} %leaf_hbm.1, f32[1,256,512]{2,1,0:T(8,128)} %prow_hbm.1), custom_call_target="tpu_custom_call" | custom-call | tf_op jit(solution)/shard_map/fronts/pallas_call | solution.py:600
  50.9 1.8 %hand_over.1 = (f32[2,256,128]{2,1,0:T(8,128)}, f32[1,512,128]{2,1,0:T(8,128)}) custom-call(f32[2,256,128]{2,1,0:T(8,128)} %get-tuple-element.4.leaf_in, f32[1,512,128]{2,1,0:T(8,128)} %get-tuple-element.5.parent_in), custom_call_target="tpu_custom_call" | custom-call | tf_op jit(solution)/shard_map/hand_over/pallas_call | solution.py:646
